TPU v7x, 512 devices: a whole 4x8x8 slice. The times are simulated.
512 devices in a mesh: seg: 32 (over y, x), step: 16 (over z, core).
Axes of the slice: x: 4, y: 8, z: 8, core: 2. Of those that a mesh axis runs over, the one named last changes fastest.
Arguments:
- trajectory: bfloat16 [16, 4096, 1536], P('step', 'seg'), may hold values from -6 to 6
- noise: bfloat16 [4096, 1536], P('seg'), may hold values from -6 to 6
- mod_shift: float32 [16, 1536], P('step'), may hold values from -3 to 3
- mod_scale: float32 [16, 1536], P('step'), may hold values from -2.5 to 2.5
- step_size: float32 [16], P('step'), may hold values from 0.2 to 0.6
- prompt_table: float32 [8, 1536], replicated, may hold values from -6 to 6
- prompt_map: int32 [4096], P('seg'), may hold values from 0 to 7
- w_qkv: bfloat16 [1536, 2304], P(('seg', 'step')), as said below
- w_out: bfloat16 [768, 1536], P(None, 'step'), may hold values from -0.21875 to 0.21875
Outputs:
- new_trajectory: bfloat16 [16, 4096, 1536], P('step', 'seg')
Inputs may be any that keep to these rules, and one draw needn't show every extreme that they name: `w_qkv`: columns for queries, keys and values of 12 heads.
All inputs are finite; a program needn't handle non-finite values.
Results may differ from a plain program's by a relative error of at most 0.011.
Values may be sent and summed in bfloat16 or wider, within the bound.
A program may use at most 64 MiB of HBM per device.

v0:
```python
import jax
import jax.numpy as jnp
from jax import lax
from jax.sharding import PartitionSpec as P

HEAD_DIM = 64


def padded(value, sides, width):
    for axis, dim in sides:
        count, length = (lax.axis_size(axis), value.shape[dim])
        up = [(i, (i + 1) % count) for i in range(count - 1)]
        down = [(j, i) for i, j in up]
        last = lax.slice_in_dim(value, length - width, length, axis=dim)
        initial = lax.slice_in_dim(value, 0, width, axis=dim)
        before = lax.ppermute(last, axis, up)
        after = lax.ppermute(initial, axis, down)
        value = jnp.concatenate([before, value, after], axis=dim)
    return value


def carried_in(value, axis, combine, identity):
    count, here = (lax.axis_size(axis), lax.axis_index(axis))
    everything = lax.all_gather(value.astype(jnp.bfloat16), axis)
    start = jnp.broadcast_to(jnp.asarray(identity, value.dtype), value.shape)

    def step(k, before):
        reached = k < here
        new = combine(before, everything[k].astype(value.dtype))
        return jnp.where(reached, new, before)

    return lax.fori_loop(0, count, step, start)


def window_attention(queries, keys, values, first_row, frames_all):
    row_count = queries.shape[0]
    key_count = keys.shape[0]
    halo_width = (key_count - row_count) // 2
    query_pos = first_row + jnp.arange(row_count, dtype=jnp.int32)
    key_pos = first_row - halo_width + jnp.arange(key_count, dtype=jnp.int32)
    distance = key_pos[None, :] - query_pos[:, None]
    allowed = (
        (jnp.abs(distance) <= halo_width)
        & (key_pos[None, :] >= 0)
        & (key_pos[None, :] < frames_all)
    )
    head_count = queries.shape[1] // HEAD_DIM
    q_heads = queries.reshape(row_count, head_count, HEAD_DIM).transpose(1, 0, 2)
    k_heads = keys.reshape(key_count, head_count, HEAD_DIM).transpose(1, 0, 2)
    v_heads = values.reshape(key_count, head_count, HEAD_DIM).transpose(1, 0, 2)

    def one_head(pieces):
        q_head, k_head, v_head = pieces
        scores = jnp.dot(q_head, k_head.T, preferred_element_type=jnp.float32) * 0.125
        scores = jnp.where(allowed, scores, jnp.float32(-1e30))
        largest = jnp.max(scores, axis=1, keepdims=True)
        lifted = jnp.exp(scores - largest)
        weights = (lifted / jnp.sum(lifted, axis=1, keepdims=True)).astype(jnp.bfloat16)
        return jnp.dot(weights, v_head, preferred_element_type=jnp.float32).astype(jnp.bfloat16)

    attended = lax.map(one_head, (q_heads, k_heads, v_heads))
    return attended.transpose(1, 0, 2).reshape(row_count, head_count * HEAD_DIM)


def shards(
    trajectory, noise, mod_shift, mod_scale, step_size, prompt_table, prompt_map, w_qkv, w_out
):
    row_count = noise.shape[0]
    hidden_width = w_out.shape[0]
    halo_width = row_count // 2
    first_row = lax.axis_index("seg") * row_count
    frames_all = row_count * lax.axis_size("seg")
    onehot = (
        prompt_map[:, None] == jnp.arange(prompt_table.shape[0], dtype=jnp.int32)[None, :]
    ).astype(jnp.float32)
    chosen = jnp.dot(onehot, prompt_table, precision=lax.Precision.HIGHEST)
    inputs = trajectory[0].astype(jnp.float32) + chosen
    center = jnp.mean(inputs, axis=-1, keepdims=True)
    spread = jnp.mean(jnp.square(inputs - center), axis=-1, keepdims=True)
    normed = (inputs - center) * lax.rsqrt(spread + 1e-06)
    modulated = (normed * (1.0 + mod_scale[0]) + mod_shift[0]).astype(jnp.bfloat16)
    projected = jnp.dot(
        modulated,
        lax.all_gather(w_qkv, ("seg", "step"), axis=0, tiled=True),
        preferred_element_type=jnp.float32,
    )
    qkv = projected.astype(jnp.bfloat16)
    queries = qkv[:, :hidden_width]
    keyval = padded(qkv[:, hidden_width:], (("seg", 0),), halo_width)
    attended = window_attention(
        queries, keyval[:, :hidden_width], keyval[:, hidden_width:], first_row, frames_all
    )
    drift_field = jnp.dot(
        attended,
        lax.all_gather(w_out, "step", axis=1, tiled=True),
        preferred_element_type=jnp.float32,
    )
    scaled = step_size[0] * drift_field

    def add_terms(earlier, later):
        return earlier + later

    prefix = carried_in(scaled, "step", add_terms, jnp.zeros(scaled.shape, jnp.float32))
    updated = (noise.astype(jnp.float32) + prefix).astype(jnp.bfloat16)
    return updated[None]


def solution(mesh):
    return jax.shard_map(
        shards,
        mesh=mesh,
        in_specs=(
            P("step", "seg", None),
            P("seg", None),
            P("step", None),
            P("step", None),
            P("step"),
            P(),
            P("seg"),
            P(("seg", "step"), None),
            P(None, "step"),
        ),
        out_specs=P("step", "seg", None),
        check_vma=False,
    )
```

profile of v0, /device:TPU:1, one launch (start us, length us, event | category | flops | bytes accessed | tf_op | source)
XLA Modules:
  0.0 272.1 jit_solution(17384112922793281116)
XLA Ops:
  6.5 0.7 all-gather.10.cloned.1.call-update
  7.3 0.7 all-gather.6.cloned.1.call-update
  8.7 0.7 add_reduce_fusion
  9.5 1.6 fusion.30
  11.1 0.2 multiply_reduce_fusion
  11.3 0.7 reduce.1
  12.1 134.7 %all-gather.10.cloned.1.call-done = bf16[512,3,2304]{2,1,0:T(4,128)(2,1)} async-done(((bf16[1,3,2304]{2,1,0:T(4,128)(2,1)}), bf16[512,3,2304]{2,1,0:T(4,128)(2,1)}) %all-gather.10.cloned.1.call-update) | async-done | bytes 7077904 | tf_op jit(solution)/shard_map/all_gather | solution.py:84
  146.8 17.0 %reshape.55 = bf16[1536,2304]{1,0:T(8,128)(2,1)} reshape(bf16[512,3,2304]{2,1,0:T(4,128)(2,1)} %all-gather.10.cloned.1.call-done) | data formatting | bytes 14155776
  163.8 4.3 %convolution_convert_fusion.1 = bf16[128,2304]{1,0:T(8,128)(2,1)S(1)} fusion(bf16[1536,2304]{1,0:T(8,128)(2,1)} %reshape.55, f32[128,1536]{1,0:T(8,128)S(1)} %get-tuple-element.208, f32[1536]{0:T(1024)S(1)} %reduce.1, f32[1536]{0:T(1024)S(1)} %add_reduce_fusion, f32[128]{0:T(128)S(1)} %add_rsqrt_fusion, f32[128]{0:T(128)S(1)} %broadcast_multiply_fusion), kind=kOutput, calls=%fused_computation.23 | convolution fusion | flops 907247616 | bytes 8467456 | tf_op jit(solution)/shard_map/dot_general | solution.py:82
  168.1 1.7 collective-permute-start
  169.8 1.3 collective-permute-start.1
  171.4 2.5 collective-permute-done
  173.9 3.9 %collective-permute-done.1 = bf16[64,1536]{1,0:T(8,128)(2,1)S(1)} collective-permute-done((bf16[64,1536]{1,0:T(8,128)(2,1)S(1)}, bf16[64,1536]{1,0:T(8,128)(2,1)S(1)}, u32[]{:S(2)}, u32[]{:S(2)}) %collective-permute-start.1) | collective-permute-done | bytes 196640 | tf_op jit(solution)/shard_map/ppermute | solution.py:17
  178.3 8.9 %while.25 = (s32[]{:T(128)}, bf16[12,128,64]{1,2,0:T(8,128)(2,1)S(1)}, bf16[12,128,64]{1,2,0:T(8,128)(2,1)S(1)}, bf16[12,256,64]{1,2,0:T(8,128)(2,1)S(1)}, bf16[...) while((s32[]{:T(128)}, ...), condition=%wide.region_5.6_spmd.clone, body=%wide.region_2.5_spmd.clone.sunk | while | flops 8822530 | bytes 498797 | solution.py:61
  178.3 0.3 fusion.40
  178.6 0.2 fusion.41
  178.8 0.2 fusion.42
  179.1 0.3 fusion.40
  179.4 0.2 fusion.41
  179.6 0.2 fusion.42
  179.8 0.3 fusion.40
  180.1 0.2 fusion.41
  180.3 0.2 fusion.42
  180.5 0.3 fusion.40
  180.9 0.2 fusion.41
  181.0 0.2 fusion.42
  181.3 0.3 fusion.40
  181.8 0.2 fusion.42
  182.0 0.3 fusion.40
  182.5 0.2 fusion.42
  182.8 0.3 fusion.40
  183.3 0.2 fusion.42
  183.5 0.3 fusion.40
  183.8 0.2 fusion.41
  184.0 0.2 fusion.42
  184.3 0.3 fusion.40
  184.8 0.2 fusion.42
  185.0 0.3 fusion.40
  185.5 0.2 fusion.42
  185.7 0.3 fusion.40
  186.2 0.2 fusion.42
  186.5 0.3 fusion.40
  187.0 0.2 fusion.42
  187.2 0.7 all-gather.6.cloned.1.call-done
  187.9 3.3 %fusion.18 = bf16[128,1536]{1,0:T(8,128)(2,1)} fusion(bf16[128,768]{0,1:T(8,128)(2,1)S(1)} %bitcast.61, bf16[768,1536]{0,1:T(8,128)(2,1)} %all-gather.6.cloned.1.call-done, f32[]{:T(128)} %bitcast.57), kind=kOutput, calls=%fused_computation.26 | convolution fusion | flops 302383104 | bytes 2949124 | tf_op jit(solution)/shard_map/dot_general | solution.py:93
  191.3 50.3 %all-gather.8.cloned.1.call-done = bf16[2048,1536]{1,0:T(8,128)(2,1)} async-done(((bf16[128,1536]{1,0:T(8,128)(2,1)}), bf16[2048,1536]{1,0:T(8,128)(2,1)}) %all-gather.8.cloned.1.call-update) | async-done | bytes 6291472 | tf_op jit(solution)/shard_map/all_gather | solution.py:24
  241.6 23.1 %while.26 = (s32[]{:T(128)}, f32[128,1536]{1,0:T(8,128)S(1)}, s32[]{:T(128)}, bf16[16,128,1536]{2,1,0:T(8,128)(2,1)}, s32[]{:T(128)}, /*index=5*/s32[]{:T(128)}) while((s32[]{:T(128)}, f32[128,1536]{1,0:T(8,128)S(1)}, s32[]{:T(128)}, bf16[16,128,1536]{2,1,0:T(8,128)(2,1)}, s32[]{:T(128)}, /*index=5*/s32[]{:T(128)}) %tuple.69), condition=%wide.region_7.8_spmd.clone, body=%wide.region_6.7_spmd.clone.sunk | while | flops 786436 | bytes 1966181 | solution.py:32
  241.6 1.5 add_select_fusion.2
  243.1 1.4 add_select_fusion.2
  244.6 1.4 add_select_fusion.2
  246.0 1.4 add_select_fusion.2
  247.5 1.4 add_select_fusion.2
  248.9 1.4 add_select_fusion.2
  250.3 1.4 add_select_fusion.2
  251.8 1.4 add_select_fusion.2
  253.2 1.4 add_select_fusion.2
  254.7 1.4 add_select_fusion.2
  256.1 1.4 add_select_fusion.2
  257.6 1.4 add_select_fusion.2
  259.0 1.4 add_select_fusion.2
  260.4 1.4 add_select_fusion.2
  261.9 1.4 add_select_fusion.2
  263.3 1.4 add_select_fusion.2
  264.8 0.8 fusion.19
  (30 shorter events, 2.1 us)
Async XLA Ops:
  6.5 2.9 %copy-start = (f32[8,1536]{1,0:T(8,128)S(1)}, f32[8,1536]{1,0:T(8,128)}, u32[]{:S(2)}) copy-start(f32[8,1536]{1,0:T(8,128)} %param.18) | copy-start | bytes 147460
  6.5 140.3 %all-gather.10.cloned.1.call-start = ((), (), s32[]{:S(2)}) async-start(), calls=%async_computation.2 | async-start | bytes 9455616 | tf_op jit(solution)/shard_map/all_gather | solution.py:84
  7.3 180.7 %all-gather.6.cloned.1.call-start = ((), (), s32[]{:S(2)}) async-start(), calls=%async_computation | async-start | bytes 2506752 | tf_op jit(solution)/shard_map/all_gather | solution.py:95
  8.0 233.6 %all-gather.8.cloned.1.call-start = ((), (), s32[]{:S(2)}) async-start(), calls=%async_computation.1 | async-start | bytes 6684672 | tf_op jit(solution)/shard_map/all_gather | solution.py:24
  168.1 5.8 %collective-permute-start = (bf16[64,1536]{1,0:T(8,128)(2,1)S(1)}, bf16[64,1536]{1,0:T(8,128)(2,1)S(1)}, u32[]{:S(2)}, u32[]{:S(2)}) collective-permute-start(bf16[64,1536]{1,0:T(8,128)(2,1)S(1)} %get-tuple-element.205), channel_id=1, source_target_pairs={{0,16},{16,32},{32,48},{48,64},{64,80},{80,96},{96,112},{112,128},... | collective-permute-start | bytes 589832 | tf_op jit(solution)/shard_map/ppermute | solution.py:16
  169.8 8.0 %collective-permute-start.1 = (bf16[64,1536]{1,0:T(8,128)(2,1)S(1)}, bf16[64,1536]{1,0:T(8,128)(2,1)S(1)}, u32[]{:S(2)}, u32[]{:S(2)}) collective-permute-start(bf16[64,1536]{1,0:T(8,128)(2,1)S(1)} %get-tuple-element.206), channel_id=1, source_target_pairs={{16,0},{32,16},{48,32},{64,48},{80,64},{96,80},{112,96},{128,112},... | collective-permute-start | bytes 589832 | tf_op jit(solution)/shard_map/ppermute | solution.py:17
  241.6 23.1 %copy-start.1 = (bf16[128,1536]{1,0:T(8,128)(2,1)S(1)}, bf16[128,1536]{1,0:T(8,128)(2,1)}, u32[]{:S(2)}) copy-start(bf16[128,1536]{1,0:T(8,128)(2,1)} %param.14) | copy-start | bytes 1179652
Sparse Core Ops, SparseCore 0:
  12.0 134.8 all-gather.9
  148.9 38.9 all-gather.5
  191.4 50.1 all-gather.7
where the time goes:
time: 273 us; the launch traced here: 272 us
  waiting for transfers between devices  194 us (71%)
  other arithmetic  27.6 us (10%)
  local copies, waits for them, and re-layouts  17.7 us (6%)
  matrix products  15.7 us (6%)
  between operations  13.9 us (5%)
  starting transfers between devices  3.06 us (1%)
    all_gather x1, waiting for transfers between devices, shards(): lax.all_gather(w_qkv, ('seg', 'step'), axis=0, tiled=True)  135 us
    all_gather x1, waiting for transfers between devices, carried_in(): everything = lax.all_gather(value.astype(jnp.bfloat16), axis)  50.3 us
    select_n x16, other arithmetic, step(): return jnp.where(reached, new, before)  22.8 us
    unnamed x5, local copies, waits for them, and re-layouts  17 us
  transfers between devices with their start and end apart: 5, of which 5 were waited for; matrix products, arithmetic and copies ran while one was open for 13% of the time, Pallas kernels for 0%

commit v1 on v0

v1 whole, which is shorter than its diff:
```python
import functools

import jax
import jax.numpy as jnp
from jax import lax
from jax.experimental import pallas as pl
from jax.experimental.pallas import tpu as pltpu
from jax.sharding import PartitionSpec as P

MESH = pl.DeviceIdType.MESH
BF16 = jnp.bfloat16
F32 = jnp.float32
XN, YN, ZN = 4, 8, 8
SEGS, STEPS = XN * YN, 2 * ZN
ROWS, HALO, D, HQ = 128, 64, 1536, 768
KEYS = ROWS + 2 * HALO
HALF = HQ // 2
CHUNKS = 9
SHARD = 3
BLOCK = SHARD * STEPS
SLOT = 32
CUT = 512
WO = D // STEPS
SEMS = 160


def dot(a, b, contract=((1,), (0,)), precision=None):
    return lax.dot_general(a, b, (contract, ((), ())), preferred_element_type=F32, precision=precision)


class Net:
    def __init__(self, send, recv):
        self.sems, self.index, self.sent = (send, recv), {}, []

    def copy(self, key, src, dst, device):
        at = self.index.setdefault(key, len(self.index))
        send, recv = self.sems
        return pltpu.make_async_remote_copy(
            src_ref=src, dst_ref=dst, send_sem=send.at[at], recv_sem=recv.at[at], device_id=device, device_id_type=MESH
        )

    def send(self, key, src, dst, device):
        copy = self.copy(key, src, dst, device)
        copy.start()
        self.sent.append(copy)

    def wait(self, key, ref, device):
        self.copy(key, ref, ref, device).wait_recv()

    def finish(self):
        for copy in self.sent:
            copy.wait_send()


def kernel(
    traj, noise, shift, scale, size, table, pmap, wq, wo, out,
    stage, shard, slots, perm, w, wt, mod, sizes, q, k, v, own_t, parts, sums, before, give, full, send, recv,
):
    seg, step = lax.axis_index("seg"), lax.axis_index("step")
    x, y, core, z = lax.rem(seg, XN), lax.div(seg, XN), lax.rem(step, 2), lax.div(step, 2)
    net = Net(send, recv)

    def ring(i, n):
        return lax.rem(i + n, n)

    def seg_of(dx, dy):
        return ring(y + dy, YN) * XN + ring(x + dx, XN)

    def at_seg(dx, dy):
        return (seg_of(dx, dy), step)

    def at_z(dz):
        return (seg, ring(z + dz, ZN) * 2 + core)

    sibling = (seg, z * 2 + 1 - core)
    following, preceding = (ring(seg + 1, SEGS), step), (ring(seg - 1, SEGS), step)

    peers = [(seg, ring(step + i, STEPS)) for i in range(1, STEPS)]
    peers += [at_seg(i, 0) for i in range(1, XN)] + [at_seg(0, 1), at_seg(0, -1), following, preceding]
    barrier = pltpu.get_barrier_semaphore()
    for peer in peers:
        pl.semaphore_signal(barrier, inc=1, device_id=peer, device_id_type=MESH)

    rows = wq[...].astype(F32)
    stage[...] = jnp.zeros_like(stage)
    for half in range(2):
        for c in range(CHUNKS):
            col = ((c // 3) * 6 + half * 3 + c % 3) * 128
            stage[half, c * SHARD : (c + 1) * SHARD, :] = rows[:, col : col + 128]
    shard[...] = stage[...].astype(BF16)
    pl.semaphore_wait(barrier, len(peers))

    for dz in range(ZN):
        for other in range(2):
            if (dz, other) == (0, 0):
                continue
            there = lax.rem(core + other, 2)
            net.send(
                ("z", dz, other), shard.at[there], slots.at[step], (seg, ring(z + dz, ZN) * 2 + there)
            )
    slots[step] = shard[core]

    onehot = (lax.broadcasted_iota(jnp.int32, (8, ROWS), 0) == pmap[...]).astype(F32)
    chosen = dot(onehot, table[...], ((0,), (0,)), lax.Precision.HIGHEST)
    inputs = traj[0].astype(F32) + chosen
    center = jnp.mean(inputs, axis=-1, keepdims=True)
    inputs = inputs - center
    spread = jnp.mean(jnp.square(inputs), axis=-1, keepdims=True)
    normed = inputs * lax.rsqrt(spread + 1e-06)
    mod[core, HALO : HALO + ROWS, :] = (normed * (1.0 + scale[...]) + shift[...]).astype(BF16)
    sizes[core] = jnp.full((8, 128), size[0], F32)

    mine, low, high = (slice(HALO, HALO + ROWS), slice(HALO, 2 * HALO), slice(ROWS, ROWS + HALO))
    first, last = slice(0, HALO), slice(HALO + ROWS, KEYS)
    net.send("up", mod.at[core, high], mod.at[core, first], following)
    net.send("down", mod.at[core, low], mod.at[core, last], preceding)
    net.send("own", mod.at[core, mine], mod.at[core, mine], sibling)
    net.send("size", sizes.at[core], sizes.at[core], sibling)

    shape = (BLOCK, STEPS * SLOT)
    i = lax.broadcasted_iota(jnp.int32, shape, 0)
    third = lax.shift_right_logical(i * 43, 7)
    j = lax.broadcasted_iota(jnp.int32, shape, 1) - third * SLOT - (i - third * SHARD)
    for c in range(CHUNKS):
        perm[c * BLOCK : (c + 1) * BLOCK, :] = jnp.where(j == c * SHARD, 1.0, 0.0).astype(BF16)
    for dz in range(ZN):
        for other in range(2):
            if (dz, other) == (0, 0):
                continue
            source = ring(z - dz, ZN) * 2 + lax.rem(core + other, 2)
            net.wait(("z", dz, other), slots.at[source], sibling)
    block = dot(perm[...], slots[...].reshape(STEPS * SLOT, 128)).astype(BF16)

    def w_rows(dx, dy):
        return pl.ds(pl.multiple_of(seg_of(dx, dy) * BLOCK, BLOCK), BLOCK)

    for c in range(CHUNKS):
        w[w_rows(0, 0), c * 128 : (c + 1) * 128] = block[c * BLOCK : (c + 1) * BLOCK]

    def part_a(dx, dy):
        return w.at[w_rows(dx, dy), 0:CUT]

    def part_b(dx, dy):
        return w.at[w_rows(dx, dy), CUT : CHUNKS * 128]

    def send_ax(dx, way):
        net.send(("ax", (dx - way) % XN), part_a(dx, 0), part_a(dx, 0), at_seg(way, 0))

    def wait_ax(dx):
        net.wait(("ax", dx % XN), part_a(dx, 0), sibling)

    def goes(way, far, is_b, dx=0):
        if far < YN // 2:
            return True
        return far == YN // 2 and (way == 1) == (is_b or dx == 0)

    def send_ay(dx, way, far):
        if goes(way, far + 1, False, dx):
            ref = part_a(dx, -way * far)
            net.send(("ay", dx, way, far + 1), ref, ref, at_seg(0, way))

    def wait_ay(dx, way, far):
        net.wait(("ay", dx, way, far), part_a(dx, -way * far), sibling)

    def send_by(way, far):
        if goes(way, far + 1, True):
            ref = part_b(0, -way * far)
            net.send(("by", way, far + 1), ref, ref, at_seg(0, way))

    def wait_by(way, far):
        net.wait(("by", way, far), part_b(0, -way * far), sibling)

    def send_bx(dx, dy, way):
        ref = part_b(dx, dy)
        net.send(("bx", dy, (dx - way) % XN), ref, ref, at_seg(way, 0))

    def wait_bx(dx, dy):
        net.wait(("bx", dy, dx % XN), part_b(dx, dy), sibling)

    def relay_bx(dy, way):
        wait_bx(-way, dy)
        send_bx(-way, dy, way)

    def wt_rows(dz, c):
        return wt.at[pl.ds(pl.multiple_of((ring(z + dz, ZN) * 2 + c) * WO, WO), WO)]

    def send_wz(way, far):
        if far + 1 < ZN // 2 or (far + 1 == ZN // 2 and way == 1):
            ref = wt_rows(-way * far, core)
            net.send(("wz", way, far + 1), ref, ref, at_z(way))

    def take_wz(way, far):
        ref = wt_rows(-way * far, core)
        net.wait(("wz", way, far), ref, sibling)
        send_wz(way, far)
        net.send(("ws", way, far), ref, ref, sibling)

    def wait_ws(way, far):
        net.wait(("ws", way, far), wt_rows(-way * far, 1 - core), sibling)

    send_ax(0, 1)
    send_ax(0, -1)
    send_by(1, 0)
    send_by(-1, 0)
    send_ay(0, 1, 0)
    send_ay(0, -1, 0)
    send_bx(0, 0, 1)
    send_bx(0, 0, -1)

    wt[pl.ds(pl.multiple_of(step * WO, WO), WO), :] = wo[...].T
    send_wz(1, 0)
    send_wz(-1, 0)
    net.send(("ws", 1, 0), wt_rows(0, core), wt_rows(0, core), sibling)

    wait_ax(-1)
    send_ax(-1, 1)
    send_ay(-1 % XN, 1, 0)
    send_ay(-1 % XN, -1, 0)
    wait_ax(1)
    send_ay(1, 1, 0)
    send_ay(1, -1, 0)
    wait_ax(2)
    send_ay(2, 1, 0)
    send_ay(2, -1, 0)
    relay_bx(0, 1)
    net.wait("up", mod.at[core, first], sibling)
    net.send("ups", mod.at[core, first], mod.at[core, first], sibling)
    net.wait("down", mod.at[core, last], sibling)
    net.send("downs", mod.at[core, last], mod.at[core, last], sibling)

    for far in range(1, YN // 2 + 1):
        for way in (1, -1):
            if goes(way, far, True):
                wait_by(way, far)
                send_by(way, far)
                send_bx(0, -way * far, 1)
                send_bx(0, -way * far, -1)
            for dx in (0, 3, 1, 2):
                if goes(way, far, False, dx):
                    wait_ay(dx, way, far)
                    send_ay(dx, way, far)
        for way in (1, -1):
            if far < ZN // 2 or way == 1:
                take_wz(way, far)
        for way in (1, -1):
            if goes(way, far, True):
                relay_bx(-way * far, way)
    for dy in range(-(YN // 2), YN // 2):
        way = -1 if dy > 0 else 1
        wait_bx(way, dy)
        wait_bx(2, dy)
    other = 1 - core
    net.wait("own", mod.at[other, mine], sibling)
    net.wait("ups", mod.at[other, first], sibling)
    net.wait("downs", mod.at[other, last], sibling)
    net.wait("size", sizes.at[other], sibling)

    for c in range(3):
        cols = slice(c * 128, (c + 1) * 128)
        k_cols = slice(HALF + c * 128, HALF + (c + 1) * 128)
        v_cols = slice(2 * HALF + c * 128, 2 * HALF + (c + 1) * 128)
        everyone = mod[...].reshape(2 * KEYS, D)
        asked = mod[:, mine, :].reshape(2 * ROWS, D)
        q[c] = (dot(asked, w[:, cols]).astype(BF16) * 0.125).astype(BF16).reshape(2, ROWS, 128)
        k[c] = dot(everyone, w[:, k_cols]).astype(BF16).reshape(2, KEYS, 128)
        v[c] = dot(everyone, w[:, v_cols]).astype(BF16).reshape(2, KEYS, 128)

    at_q = lax.broadcasted_iota(jnp.int32, (ROWS, KEYS), 0)
    at_k = lax.broadcasted_iota(jnp.int32, (ROWS, KEYS), 1)
    frame = seg * ROWS - HALO + at_k
    allowed = (at_k >= at_q) & (at_k <= at_q + 2 * HALO) & (frame >= 0) & (frame < SEGS * ROWS)
    bias = jnp.where(allowed, 0.0, -1e30).astype(F32)
    bias = jnp.concatenate([bias, bias], axis=0)
    lane = lax.broadcasted_iota(jnp.int32, (ROWS, 128), 1)
    ones = jnp.ones((KEYS, 128), BF16)
    for c in range(3):
        total = None
        for s in range(2):
            asked = q[c, s]
            nothing = jnp.zeros_like(asked)
            both = jnp.concatenate([jnp.where(lane < 64, asked, nothing), jnp.where(lane < 64, nothing, asked)], axis=0)
            scores = dot(both, k[c, s], ((1,), (1,))) + bias
            lifted = jnp.exp(scores - jnp.max(scores, axis=1, keepdims=True)).astype(BF16)
            got = dot(lifted, v[c, s]) / dot(lifted, ones)
            got = jnp.where(lane < 64, got[:ROWS], got[ROWS:]).astype(BF16)
            term = got.astype(F32) * sizes[s, 0:1, :]
            if s == 0:
                own_t[:, c * 128 : (c + 1) * 128] = term.astype(BF16)
                total = term
            else:
                total = total + term
        give[:, c * 128 : (c + 1) * 128] = total.astype(BF16)

    part = ROWS // ZN

    def part_rows(i):
        return pl.ds(pl.multiple_of(i * part, part), part)

    for dz in range(1, ZN):
        net.send(("there", dz), give.at[part_rows(ring(z + dz, ZN))], parts.at[z], at_z(dz))
    parts[z] = give[part_rows(z), :]
    for dz in range(1, ZN):
        net.wait(("there", dz), parts.at[ring(z - dz, ZN)], sibling)
    total = jnp.zeros((part, HALF), F32)
    for i in range(ZN):
        sums[i] = total.astype(BF16)
        total = total + parts[i].astype(F32)
    for dz in range(1, ZN):
        net.send(("back", dz), sums.at[ring(z + dz, ZN)], before.at[part_rows(z)], at_z(dz))
    before[part_rows(z), :] = sums[z]
    for dz in range(1, ZN):
        net.wait(("back", dz), before.at[part_rows(ring(z - dz, ZN))], sibling)

    even = before[...]
    odd = (even.astype(F32) + own_t[...].astype(F32)).astype(BF16)
    full[core] = jnp.where(core == 0, even, odd)
    sums_there = jnp.where(core == 0, odd, even)
    own_t[...] = sums_there
    net.send("full", own_t, full.at[core], sibling)
    for far in range(0, ZN // 2 + 1):
        for way in (1, -1):
            if (far > 0 or way == 1) and (far < ZN // 2 or way == 1):
                wait_ws(way, far)
    net.wait("full", full.at[other], sibling)
    drift = dot(full[0], wt[:, 0:HALF], ((1,), (1,))) + dot(full[1], wt[:, HALF:HQ], ((1,), (1,)))
    out[...] = (noise[...].astype(F32) + drift).astype(BF16)
    net.finish()


def shards(trajectory, noise, mod_shift, mod_scale, step_size, prompt_table, prompt_map, w_qkv, w_out):
    vmem = pl.BlockSpec(memory_space=pltpu.VMEM)
    smem = pl.BlockSpec(memory_space=pltpu.SMEM)
    result = pl.pallas_call(
        kernel,
        out_shape=jax.ShapeDtypeStruct((ROWS, D), BF16),
        in_specs=[vmem, vmem, vmem, vmem, smem, vmem, vmem, vmem, vmem],
        out_specs=vmem,
        scratch_shapes=[
            pltpu.VMEM((2, SLOT, 128), F32),
            pltpu.VMEM((2, SLOT, 128), BF16),
            pltpu.VMEM((STEPS, SLOT, 128), BF16),
            pltpu.VMEM((CHUNKS * BLOCK, STEPS * SLOT), BF16),
            pltpu.VMEM((D, CHUNKS * 128), BF16),
            pltpu.VMEM((D, HQ), BF16),
            pltpu.VMEM((2, KEYS, D), BF16),
            pltpu.VMEM((2, 8, 128), F32),
            pltpu.VMEM((3, 2, ROWS, 128), BF16),
            pltpu.VMEM((3, 2, KEYS, 128), BF16),
            pltpu.VMEM((3, 2, KEYS, 128), BF16),
            pltpu.VMEM((ROWS, HALF), BF16),
            pltpu.VMEM((ZN, ROWS // ZN, HALF), BF16),
            pltpu.VMEM((ZN, ROWS // ZN, HALF), BF16),
            pltpu.VMEM((ROWS, HALF), BF16),
            pltpu.VMEM((ROWS, HALF), BF16),
            pltpu.VMEM((2, ROWS, HALF), BF16),
            pltpu.SemaphoreType.DMA((SEMS,)),
            pltpu.SemaphoreType.DMA((SEMS,)),
        ],
        compiler_params=pltpu.CompilerParams(
            collective_id=0, has_side_effects=True, vmem_limit_bytes=48 * 1024 * 1024
        ),
    )(
        trajectory, noise, mod_shift, mod_scale, step_size, prompt_table,
        prompt_map.reshape(1, ROWS), w_qkv, w_out,
    )
    return result[None]


def solution(mesh):
    return jax.shard_map(
        shards,
        mesh=mesh,
        in_specs=(
            P("step", "seg", None),
            P("seg", None),
            P("step", None),
            P("step", None),
            P("step"),
            P(),
            P("seg"),
            P(("seg", "step"), None),
            P(None, "step"),
        ),
        out_specs=P("step", "seg", None),
        check_vma=False,
    )
```

time: 273 us -> 79.7 us (0.29)
  waiting for transfers between devices: 194 us -> 0 us
  Pallas kernels: 0 us -> 74.9 us
  other arithmetic: 27.6 us -> 0 us
  matrix products: 15.7 us -> 0 us
  local copies, waits for them, and re-layouts: 17.7 us -> 3.86 us
  between operations: 13.9 us -> 0.75 us
  starting transfers between devices: 3.06 us -> 0 us
    all_gather x3 -> x0, waiting for transfers between devices: 186 us -> none  [the longest x1 135 us: shards(): lax.all_gather(w_qkv, ('seg', 'step'), axis=0, tiled=True)]
    pallas_call x0 -> x1, Pallas kernels: none -> 74.9 us  [shards(): pl.pallas_call(kernel, out_shape=jax.ShapeDtypeStruct((ROWS, D), BF16), i...]
    select_n x16 -> x0, other arithmetic: 22.8 us -> none  [step(): return jnp.where(reached, new, before)]
    dot_general x27 -> x0, matrix products: 15.7 us -> none  [the longest x1 4.25 us: shards(): jnp.dot(modulated, lax.all_gather(w_qkv, ('seg', 'step'), axis=0, tiled=T...]
    unnamed x5 -> x16, local copies, waits for them, and re-layouts: 17 us -> 3.86 us
    ppermute x2 -> x0, waiting for transfers between devices: 6.45 us -> none  [the longest x1 3.9 us: padded(): after = lax.ppermute(initial, axis, down)]
    ppermute x2 -> x0, starting transfers between devices: 2.98 us -> none  [the longest x1 1.69 us: padded(): before = lax.ppermute(last, axis, up)]
  transfers between devices with their start and end apart: 5 -> 0, of which waited for: 5 -> 0; matrix products, arithmetic and copies ran while one was open for 13% -> 0% of each run, Pallas kernels for 0% -> 0%
where the time goes in v1:
time: 79.7 us; the launch traced here: 79.5 us
  Pallas kernels  74.9 us (94%)
  local copies, waits for them, and re-layouts  3.86 us (5%)
    pallas_call x1, Pallas kernels, shards(): pl.pallas_call(kernel, out_shape=jax.ShapeDtypeStruct((ROWS, D), BF16), i...  74.9 us
    unnamed x16, local copies, waits for them, and re-layouts  3.86 us

profile of v1, /device:TPU:1, one launch (start us, length us, event | category | flops | bytes accessed | tf_op | source)
XLA Modules:
  0.0 79.5 jit_solution(16453285629671156708)
XLA Ops:
  0.7 0.0 copy-start.2
  0.7 0.0 copy-start.3
  0.7 0.0 copy-start.4
  0.7 0.0 copy-start.5
  0.7 0.0 copy-start.6
  0.7 1.1 %copy.10.wo = bf16[768,96]{1,0:T(8,128)(2,1)S(1)} copy(bf16[768,96]{0,1:T(8,128)(2,1)} %param.17) | data formatting | bytes 294912 | tf_op args[8]
  1.8 0.0 copy-done.2
  1.8 0.0 copy-done.3
  1.8 0.0 copy-done.4
  1.8 0.0 copy-done.5
  1.9 0.0 copy-done.6
  1.9 0.0 copy-start
  1.9 1.0 %copy-done = bf16[1,128,1536]{2,1,0:T(8,128)(2,1)S(1)} copy-done((bf16[1,128,1536]{2,1,0:T(8,128)(2,1)S(1)}, bf16[1,128,1536]{2,1,0:T(8,128)(2,1)}, u32[]{:S(2)}) %copy-start) | copy-done | bytes 393240
  2.9 0.0 copy-start.1
  2.9 1.0 %copy-done.1 = bf16[128,1536]{1,0:T(8,128)(2,1)S(1)} copy-done((bf16[128,1536]{1,0:T(8,128)(2,1)S(1)}, bf16[128,1536]{1,0:T(8,128)(2,1)}, u32[]{:S(2)}) %copy-start.1) | copy-done | bytes 393240
  3.9 74.9 %shard_map.91 = bf16[128,1536]{1,0:T(8,128)(2,1)S(1)} custom-call(bf16[1,128,1536]{2,1,0:T(8,128)(2,1)S(1)} %copy-done, bf16[128,1536]{1,0:T(8,128)(2,1)S(1)} %copy-done.1, f32[1,1536]{1,0:T(1,128)S(1)} %copy-done.4, f32[1,1536]{1,0:T(1,128)S(1)} %copy-done.5, f32[1]{0:T(128)S(6)} %copy.12.size, f32[8,1536]{1,0:T(8,128)S(1)} %copy-done.2, ...), custom_call_target="tpu_custom_call" | custom-call | tf_op jit(solution)/shard_map/pallas_call | solution.py:333
  78.8 0.7 copy.13
Async XLA Ops:
  0.7 1.2 %copy-start.2 = (f32[8,1536]{1,0:T(8,128)S(1)}, f32[8,1536]{1,0:T(8,128)}, u32[]{:S(2)}) copy-start(f32[8,1536]{1,0:T(8,128)} %table.1) | copy-start | bytes 147460
  0.7 1.2 %copy-start.3 = (bf16[3,2304]{1,0:T(4,128)(2,1)S(1)}, bf16[3,2304]{1,0:T(4,128)(2,1)}, u32[]{:S(2)}) copy-start(bf16[3,2304]{1,0:T(4,128)(2,1)} %wq.1) | copy-start | bytes 41476
  0.7 1.2 %copy-start.4 = (f32[1,1536]{1,0:T(1,128)S(1)}, f32[1,1536]{1,0:T(1,128)}, u32[]{:S(2)}) copy-start(f32[1,1536]{1,0:T(1,128)} %shift.1) | copy-start | bytes 18436
  0.7 1.2 %copy-start.5 = (f32[1,1536]{1,0:T(1,128)S(1)}, f32[1,1536]{1,0:T(1,128)}, u32[]{:S(2)}) copy-start(f32[1,1536]{1,0:T(1,128)} %scale.1) | copy-start | bytes 18436
  0.7 1.2 %copy-start.6 = (s32[128]{0:T(128)S(1)}, s32[128]{0:T(128)}, u32[]{:S(2)}) copy-start(s32[128]{0:T(128)} %param.15) | copy-start | bytes 1540
  1.9 1.0 %copy-start = (bf16[1,128,1536]{2,1,0:T(8,128)(2,1)S(1)}, bf16[1,128,1536]{2,1,0:T(8,128)(2,1)}, u32[]{:S(2)}) copy-start(bf16[1,128,1536]{2,1,0:T(8,128)(2,1)} %traj.1) | copy-start | bytes 1179652
  2.9 1.0 %copy-start.1 = (bf16[128,1536]{1,0:T(8,128)(2,1)S(1)}, bf16[128,1536]{1,0:T(8,128)(2,1)}, u32[]{:S(2)}) copy-start(bf16[128,1536]{1,0:T(8,128)(2,1)} %noise.1) | copy-start | bytes 1179652

commit v2 on v1

v2 whole, which is shorter than its diff:
```python
import functools

import jax
import jax.numpy as jnp
from jax import lax
from jax.experimental import pallas as pl
from jax.experimental.pallas import tpu as pltpu
from jax.sharding import PartitionSpec as P

MESH = pl.DeviceIdType.MESH
BF16 = jnp.bfloat16
F32 = jnp.float32
XN, YN, ZN = 4, 8, 8
SEGS, STEPS = XN * YN, 2 * ZN
ROWS, HALO, D, HQ = 128, 64, 1536, 768
KEYS = ROWS + 2 * HALO
HALF = HQ // 2
CHUNKS = 9
SHARD = 3
BLOCK = SHARD * STEPS
SLOT = 32
WO = D // STEPS
PAIR = 2 * XN * BLOCK
SEMS = 160


def dot(a, b, contract=((1,), (0,)), precision=None):
    return lax.dot_general(a, b, (contract, ((), ())), preferred_element_type=F32, precision=precision)


class Net:
    def __init__(self, send, recv):
        self.sems, self.index, self.sent = (send, recv), {}, []

    def copy(self, key, src, dst, device):
        at = self.index.setdefault(key, len(self.index))
        send, recv = self.sems
        return pltpu.make_async_remote_copy(
            src_ref=src, dst_ref=dst, send_sem=send.at[at], recv_sem=recv.at[at], device_id=device, device_id_type=MESH
        )

    def send(self, key, src, dst, device):
        copy = self.copy(key, src, dst, device)
        copy.start()
        self.sent.append(copy)

    def wait(self, key, ref, device):
        self.copy(key, ref, ref, device).wait_recv()

    def finish(self):
        for copy in self.sent:
            copy.wait_send()


def kernel(
    traj_hbm, noise_hbm, shift_hbm, scale_hbm, size, table_hbm, pmap_hbm, wq_hbm, wo_hbm, out,
    traj, noise, shift, scale, table, pmap, wq, stage, shard, slots, perm, w, wt, mod, sizes,
    sum_q, sum_kv, q, k, v, own_t, parts, sums, before, give, full, load, send, recv,
):
    seg, step = lax.axis_index("seg"), lax.axis_index("step")
    x, y, core, z = lax.rem(seg, XN), lax.div(seg, XN), lax.rem(step, 2), lax.div(step, 2)
    other = 1 - core
    net = Net(send, recv)

    def ring(i, n):
        return lax.rem(i + n, n)

    def seg_of(dx, dy):
        return ring(y + dy, YN) * XN + ring(x + dx, XN)

    def at_seg(dx, dy):
        return (seg_of(dx, dy), step)

    def at_z(dz):
        return (seg, ring(z + dz, ZN) * 2 + core)

    sibling = (seg, z * 2 + other)
    following, preceding = (ring(seg + 1, SEGS), step), (ring(seg - 1, SEGS), step)

    peers = [(seg, ring(step + i, STEPS)) for i in range(1, STEPS)]
    peers += [at_seg(i, 0) for i in range(1, XN)] + [at_seg(0, 1), at_seg(0, -1), following, preceding]
    barrier = pltpu.get_barrier_semaphore()
    for peer in peers:
        pl.semaphore_signal(barrier, inc=1, device_id=peer, device_id_type=MESH)

    def wt_rows(dz, c):
        return wt.at[pl.ds(pl.multiple_of((ring(z + dz, ZN) * 2 + c) * WO, WO), WO)]

    loads = [
        pltpu.make_async_copy(src, dst, load.at[i])
        for i, (src, dst) in enumerate(
            [
                (wq_hbm, wq), (traj_hbm, traj), (pmap_hbm, pmap), (table_hbm, table), (shift_hbm, shift),
                (scale_hbm, scale), (wo_hbm, wt_rows(0, core)), (noise_hbm, noise),
            ]
        )
    ]
    for copy in loads:
        copy.start()

    stage[...] = jnp.zeros_like(stage)
    loads[0].wait()
    rows = wq[...].astype(F32)
    for half in range(2):
        for c in range(CHUNKS):
            col = ((c // 3) * 6 + half * 3 + c % 3) * 128
            stage[half, c * SHARD : (c + 1) * SHARD, :] = rows[:, col : col + 128]
    shard[...] = stage[...].astype(BF16)
    slots[step] = shard[core]
    pl.semaphore_wait(barrier, len(peers))

    for dz in (4, 3, 5, 2, 6, 1, 7, 0):
        for swap in range(2):
            if (dz, swap) == (0, 0):
                continue
            there = lax.rem(core + swap, 2)
            net.send(("z", dz, swap), shard.at[there], slots.at[step], (seg, ring(z + dz, ZN) * 2 + there))

    shape = (BLOCK, STEPS * SLOT)
    i = lax.broadcasted_iota(jnp.int32, shape, 0)
    third = lax.shift_right_logical(i * 43, 7)
    j = lax.broadcasted_iota(jnp.int32, shape, 1) - third * SLOT - (i - third * SHARD)
    for c in range(CHUNKS):
        perm[c * BLOCK : (c + 1) * BLOCK, :] = jnp.where(j == c * SHARD, 1.0, 0.0).astype(BF16)
    for dz in range(ZN):
        for swap in range(2):
            if (dz, swap) == (0, 0):
                continue
            source = ring(z - dz, ZN) * 2 + lax.rem(core + swap, 2)
            net.wait(("z", dz, swap), slots.at[source], sibling)
    block = dot(perm[...], slots[...].reshape(STEPS * SLOT, 128)).astype(BF16)

    ours = 1 + lax.rem(z, 2)

    def part(which, dx, dy):
        return w.at[which, pl.ds(pl.multiple_of(seg_of(dx, dy) * BLOCK, BLOCK), BLOCK)]

    for c in range(CHUNKS):
        own_rows = pl.ds(pl.multiple_of(seg * BLOCK, BLOCK), BLOCK)
        w[c // 3, own_rows, (c % 3) * 128 : (c % 3 + 1) * 128] = block[c * BLOCK : (c + 1) * BLOCK]

    def goes(way, far, is_b, dx=0):
        if far < YN // 2:
            return True
        return far == YN // 2 and (way == 1) == (is_b or dx % 2 == 0)

    def send_ax(dx, way):
        ref = part(ours, dx, 0)
        net.send(("ax", (dx - way) % XN), ref, ref, at_seg(way, 0))

    def wait_ax(dx):
        net.wait(("ax", dx % XN), part(ours, dx, 0), sibling)

    def send_ay(dx, way, far):
        if goes(way, far + 1, False, dx):
            ref = part(ours, dx, -way * far)
            net.send(("ay", dx, way, far + 1), ref, ref, at_seg(0, way))

    def wait_ay(dx, way, far):
        net.wait(("ay", dx, way, far), part(ours, dx, -way * far), sibling)

    def send_az(dx, dy):
        ref = part(ours, dx, dy)
        net.send(("az", dx, dy % YN), ref, ref, at_z(1 if dx % 2 == 0 else -1))

    def wait_az(dx, dy):
        net.wait(("az", dx, dy % YN), part(3 - ours, dx, dy), sibling)

    def send_by(way, far):
        if goes(way, far + 1, True):
            ref = part(0, 0, -way * far)
            net.send(("by", way, far + 1), ref, ref, at_seg(0, way))

    def wait_by(way, far):
        net.wait(("by", way, far), part(0, 0, -way * far), sibling)

    def send_bx(dx, dy, way):
        ref = part(0, dx, dy)
        net.send(("bx", dy, (dx - way) % XN), ref, ref, at_seg(way, 0))

    def wait_bx(dx, dy):
        net.wait(("bx", dy, dx % XN), part(0, dx, dy), sibling)

    def relay_bx(dy, way):
        wait_bx(-way, dy)
        send_bx(-way, dy, way)

    def send_wz(way, far):
        if far + 1 < ZN // 2 or (far + 1 == ZN // 2 and way == 1):
            ref = wt_rows(-way * far, core)
            net.send(("wz", way, far + 1), ref, ref, at_z(way))

    def take_wz(way, far):
        if far < ZN // 2 or way == 1:
            ref = wt_rows(-way * far, core)
            net.wait(("wz", way, far), ref, sibling)
            send_wz(way, far)
            net.send(("ws", way, far), ref, ref, sibling)

    def wait_ws(way, far):
        if (far > 0 or way == 1) and (far < ZN // 2 or way == 1):
            net.wait(("ws", way, far), wt_rows(-way * far, 1 - core), sibling)

    mine, low, high = (slice(HALO, HALO + ROWS), slice(HALO, 2 * HALO), slice(ROWS, ROWS + HALO))
    first, last = slice(0, HALO), slice(HALO + ROWS, KEYS)

    def project(pair, start):
        rows = pl.ds(pl.multiple_of(pair * PAIR, PAIR), PAIR)
        everyone = mod[:, :, rows].reshape(2 * KEYS, PAIR)
        asked = mod[:, mine, rows].reshape(2 * ROWS, PAIR)
        add_q, add_k, add_v = dot(asked, w[0, rows]), dot(everyone, w[1, rows]), dot(everyone, w[2, rows])
        sum_q[...] = add_q if start else sum_q[...] + add_q
        sum_kv[0] = add_k if start else sum_kv[0] + add_k
        sum_kv[1] = add_v if start else sum_kv[1] + add_v

    send_ax(0, 1)
    send_ax(0, -1)
    send_ay(0, 1, 0)
    send_ay(0, -1, 0)
    net.send(("ax", 2), part(ours, 0, 0), part(ours, 0, 0), at_seg(2, 0))
    send_by(1, 0)
    send_by(-1, 0)
    send_bx(0, 0, 1)
    send_bx(0, 0, -1)

    for copy in loads[1:]:
        copy.wait()
    onehot = (lax.broadcasted_iota(jnp.int32, (8, ROWS), 0) == pmap[...]).astype(F32)
    chosen = dot(onehot, table[...], ((0,), (0,)), lax.Precision.HIGHEST)
    inputs = traj[0].astype(F32) + chosen
    center = jnp.mean(inputs, axis=-1, keepdims=True)
    inputs = inputs - center
    spread = jnp.mean(jnp.square(inputs), axis=-1, keepdims=True)
    normed = inputs * lax.rsqrt(spread + 1e-06)
    mod[core, mine, :] = (normed * (1.0 + scale[...]) + shift[...]).astype(BF16)
    sizes[core] = jnp.full((8, 128), size[0], F32)

    for dx in (3, 1, 2):
        wait_ax(dx)
        send_ay(dx, 1, 0)
        send_ay(dx, -1, 0)
        send_az(dx, 0)
    net.send("up", mod.at[core, high], mod.at[core, first], following)
    net.send("down", mod.at[core, low], mod.at[core, last], preceding)
    net.send("own", mod.at[core, mine], mod.at[core, mine], sibling)
    net.send("size", sizes.at[core], sizes.at[core], sibling)
    relay_bx(0, 1)

    last_level = YN // 2
    pair = lax.div(y, 2)
    side = 1 - 2 * lax.rem(y, 2)
    pairs = [pair, ring(pair - side, YN // 2), ring(pair + side, YN // 2), ring(pair + 2, YN // 2)]

    def settle(far):
        for dy in {far % YN, -far % YN}:
            dy = dy - YN if dy >= YN // 2 else dy
            wait_bx(-1 if dy > 0 else 1, dy)
            if abs(dy) == last_level:
                wait_bx(-1, dy)
            wait_bx(2, dy)
            for dx in range(XN):
                if (dx, dy) != (0, 0):
                    wait_az(dx, dy)

    for far in range(1, last_level + 1):
        for way in (1, -1):
            if goes(way, far, True):
                wait_by(way, far)
                send_by(way, far)
                send_bx(0, -way * far, 1)
                send_bx(0, -way * far, -1)
                if far == last_level:
                    ref = part(0, 0, -way * far)
                    net.send(("bx", -way * far, 2), ref, ref, at_seg(2, 0))
        for dx in (0, 3, 1, 2):
            for way in (1, -1):
                if goes(way, far, False, dx):
                    wait_ay(dx, way, far)
                    send_ay(dx, way, far)
                    send_az(dx, -way * far)
        for way in (1, -1):
            if goes(way, far, True) and far < last_level:
                relay_bx(-way * far, way)
        if far == 1:
            net.wait("up", mod.at[core, first], sibling)
            net.send("ups", mod.at[core, first], mod.at[core, first], sibling)
            net.wait("down", mod.at[core, last], sibling)
            net.send("downs", mod.at[core, last], mod.at[core, last], sibling)
            settle(0)
        if far == 2:
            net.wait("own", mod.at[other, mine], sibling)
            net.wait("ups", mod.at[other, first], sibling)
            net.wait("downs", mod.at[other, last], sibling)
            net.wait("size", sizes.at[other], sibling)
        if far > 1:
            settle(far - 1)
            project(pairs[far - 2], far == 2)
    send_wz(1, 0)
    send_wz(-1, 0)
    net.send(("ws", 1, 0), wt_rows(0, core), wt_rows(0, core), sibling)
    settle(last_level)
    project(pairs[3], False)
    take_wz(1, 1)
    take_wz(-1, 1)
    for c in range(3):
        cols = slice(c * 128, (c + 1) * 128)
        q[c] = (sum_q[:, cols].astype(BF16) * 0.125).astype(BF16).reshape(2, ROWS, 128)
        k[c] = sum_kv[0, :, cols].astype(BF16).reshape(2, KEYS, 128)
        v[c] = sum_kv[1, :, cols].astype(BF16).reshape(2, KEYS, 128)

    at_q = lax.broadcasted_iota(jnp.int32, (ROWS, KEYS), 0)
    at_k = lax.broadcasted_iota(jnp.int32, (ROWS, KEYS), 1)
    frame = seg * ROWS - HALO + at_k
    allowed = (at_k >= at_q) & (at_k <= at_q + 2 * HALO) & (frame >= 0) & (frame < SEGS * ROWS)
    bias = jnp.where(allowed, 0.0, -1e30).astype(F32)
    bias = jnp.concatenate([bias, bias], axis=0)
    lane = lax.broadcasted_iota(jnp.int32, (ROWS, 128), 1)
    ones = jnp.ones((KEYS, 128), BF16)
    for c in range(3):
        total = None
        for s in range(2):
            asked = q[c, s]
            nothing = jnp.zeros_like(asked)
            both = jnp.concatenate([jnp.where(lane < 64, asked, nothing), jnp.where(lane < 64, nothing, asked)], axis=0)
            scores = dot(both, k[c, s], ((1,), (1,))) + bias
            lifted = jnp.exp(scores - jnp.max(scores, axis=1, keepdims=True)).astype(BF16)
            got = dot(lifted, v[c, s]) / dot(lifted, ones)
            got = jnp.where(lane < 64, got[:ROWS], got[ROWS:]).astype(BF16)
            term = got.astype(F32) * sizes[s, 0:1, :]
            if s == 0:
                own_t[:, c * 128 : (c + 1) * 128] = term.astype(BF16)
                total = term
            else:
                total = total + term
        give[:, c * 128 : (c + 1) * 128] = total.astype(BF16)
        if c == 1:
            take_wz(1, 2)
            take_wz(-1, 2)

    share = ROWS // ZN

    def share_rows(i):
        return pl.ds(pl.multiple_of(i * share, share), share)

    for dz in (4, 3, 5, 2, 6, 1, 7):
        net.send(("there", dz), give.at[share_rows(ring(z + dz, ZN))], parts.at[z], at_z(dz))
    parts[z] = give[share_rows(z), :]
    take_wz(1, 3)
    take_wz(-1, 3)
    for dz in range(1, ZN):
        net.wait(("there", dz), parts.at[ring(z - dz, ZN)], sibling)
    total = jnp.zeros((share, HALF), F32)
    for i in range(ZN):
        sums[i] = total.astype(BF16)
        total = total + parts[i].astype(F32)
    for dz in (4, 3, 5, 2, 6, 1, 7):
        net.send(("back", dz), sums.at[ring(z + dz, ZN)], before.at[share_rows(z)], at_z(dz))
    before[share_rows(z), :] = sums[z]
    take_wz(1, 4)
    for dz in range(1, ZN):
        net.wait(("back", dz), before.at[share_rows(ring(z - dz, ZN))], sibling)

    even = before[...]
    odd = (even.astype(F32) + own_t[...].astype(F32)).astype(BF16)
    full[core] = jnp.where(core == 0, even, odd)
    own_t[...] = jnp.where(core == 0, odd, even)
    net.send("full", own_t, full.at[core], sibling)
    for far in range(0, ZN // 2 + 1):
        wait_ws(1, far)
        wait_ws(-1, far)
    net.wait("full", full.at[other], sibling)
    drift = dot(full[0], wt[:, 0:HALF], ((1,), (1,))) + dot(full[1], wt[:, HALF:HQ], ((1,), (1,)))
    out[...] = (noise[...].astype(F32) + drift).astype(BF16)
    net.finish()


def shards(trajectory, noise, mod_shift, mod_scale, step_size, prompt_table, prompt_map, w_qkv, w_out):
    vmem = pl.BlockSpec(memory_space=pltpu.VMEM)
    smem = pl.BlockSpec(memory_space=pltpu.SMEM)
    hbm = pl.BlockSpec(memory_space=pl.ANY)
    result = pl.pallas_call(
        kernel,
        out_shape=jax.ShapeDtypeStruct((ROWS, D), BF16),
        in_specs=[hbm, hbm, hbm, hbm, smem, hbm, hbm, hbm, hbm],
        out_specs=vmem,
        scratch_shapes=[
            pltpu.VMEM((1, ROWS, D), BF16),
            pltpu.VMEM((ROWS, D), BF16),
            pltpu.VMEM((1, D), F32),
            pltpu.VMEM((1, D), F32),
            pltpu.VMEM((8, D), F32),
            pltpu.VMEM((1, ROWS), jnp.int32),
            pltpu.VMEM((SHARD, 3 * HQ), BF16),
            pltpu.VMEM((2, SLOT, 128), F32),
            pltpu.VMEM((2, SLOT, 128), BF16),
            pltpu.VMEM((STEPS, SLOT, 128), BF16),
            pltpu.VMEM((CHUNKS * BLOCK, STEPS * SLOT), BF16),
            pltpu.VMEM((3, D, HALF), BF16),
            pltpu.VMEM((D, HQ), BF16),
            pltpu.VMEM((2, KEYS, D), BF16),
            pltpu.VMEM((2, 8, 128), F32),
            pltpu.VMEM((2 * ROWS, HALF), F32),
            pltpu.VMEM((2, 2 * KEYS, HALF), F32),
            pltpu.VMEM((3, 2, ROWS, 128), BF16),
            pltpu.VMEM((3, 2, KEYS, 128), BF16),
            pltpu.VMEM((3, 2, KEYS, 128), BF16),
            pltpu.VMEM((ROWS, HALF), BF16),
            pltpu.VMEM((ZN, ROWS // ZN, HALF), BF16),
            pltpu.VMEM((ZN, ROWS // ZN, HALF), BF16),
            pltpu.VMEM((ROWS, HALF), BF16),
            pltpu.VMEM((ROWS, HALF), BF16),
            pltpu.VMEM((2, ROWS, HALF), BF16),
            pltpu.SemaphoreType.DMA((8,)),
            pltpu.SemaphoreType.DMA((SEMS,)),
            pltpu.SemaphoreType.DMA((SEMS,)),
        ],
        compiler_params=pltpu.CompilerParams(
            collective_id=0, has_side_effects=True, vmem_limit_bytes=60 * 1024 * 1024
        ),
    )(
        trajectory, noise, mod_shift, mod_scale, step_size, prompt_table,
        prompt_map.reshape(1, ROWS), w_qkv, w_out.T,
    )
    return result[None]


def solution(mesh):
    return jax.shard_map(
        shards,
        mesh=mesh,
        in_specs=(
            P("step", "seg", None),
            P("seg", None),
            P("step", None),
            P("step", None),
            P("step"),
            P(),
            P("seg"),
            P(("seg", "step"), None),
            P(None, "step"),
        ),
        out_specs=P("step", "seg", None),
        check_vma=False,
    )
```

time: 79.7 us -> 79.7 us (level)
  Pallas kernels: 74.9 us -> 77.1 us
  local copies, waits for them, and re-layouts: 3.86 us -> 1.77 us
    pallas_call x1, Pallas kernels: 74.9 us -> 77.1 us  [shards(): pl.pallas_call(kernel, out_shape=jax.ShapeDtypeStruct((ROWS, D), BF16), i...]
    unnamed x16 -> x1, local copies, waits for them, and re-layouts: 3.86 us -> 1.77 us
where the time goes in v2:
time: 79.7 us; the launch traced here: 79.5 us
  Pallas kernels  77.1 us (97%)
  local copies, waits for them, and re-layouts  1.77 us (2%)
    pallas_call x1, Pallas kernels, shards(): pl.pallas_call(kernel, out_shape=jax.ShapeDtypeStruct((ROWS, D), BF16), i...  77.1 us
    unnamed x1, local copies, waits for them, and re-layouts  1.77 us

profile of v2, /device:TPU:1, one launch (start us, length us, event | category | flops | bytes accessed | tf_op | source)
XLA Modules:
  0.0 79.5 jit_solution(13886964636216298953)
XLA Ops:
  0.7 77.1 %shard_map.91 = bf16[128,1536]{1,0:T(8,128)(2,1)} custom-call(bf16[1,128,1536]{2,1,0:T(8,128)(2,1)} %traj_hbm.1, bf16[128,1536]{1,0:T(8,128)(2,1)} %noise_hbm.1, f32[1,1536]{1,0:T(1,128)} %shift_hbm.1, f32[1,1536]{1,0:T(1,128)} %scale_hbm.1, f32[1]{0:T(128)S(6)} %copy.11.size, f32[8,1536]{1,0:T(8,128)} %table_hbm.1, s32[1,128]{1,0:T(1,128)} %bitcast.5, ...), custom_call_target="tpu_custom_call" | custom-call | tf_op jit(solution)/shard_map/pallas_call | solution.py:381
  77.8 1.8 %copy.12 = bf16[1,128,1536]{2,1,0:T(8,128)(2,1)} copy(bf16[1,128,1536]{2,1,0:T(8,128)(2,1)} %bitcast.3) | data formatting | bytes 786432

commit v3 on v2

v3 whole, which is shorter than its diff:
```python
import functools

import jax
import jax.numpy as jnp
from jax import lax
from jax.experimental import pallas as pl
from jax.experimental.pallas import tpu as pltpu
from jax.sharding import PartitionSpec as P

MESH = pl.DeviceIdType.MESH
BF16 = jnp.bfloat16
F32 = jnp.float32
XN, YN, ZN = 4, 8, 8
SEGS, STEPS = XN * YN, 2 * ZN
ROWS, HALO, D, HQ = 128, 64, 1536, 768
KEYS = ROWS + 2 * HALO
HALF = HQ // 2
CHUNKS = 9
SHARD = 3
BLOCK = SHARD * STEPS
SLOT = 32
WO = D // STEPS
PAIR = 2 * XN * BLOCK
SENDS, RECVS = 12, 80


def dot(a, b, contract=((1,), (0,)), precision=None):
    return lax.dot_general(a, b, (contract, ((), ())), preferred_element_type=F32, precision=precision)


class Net:
    def __init__(self, send, recv):
        self.sems, self.index, self.count = (send, recv), ({}, {}), {}

    def sem(self, side, name):
        index = self.index[side]
        return self.sems[side].at[index.setdefault(name, len(index))]

    def send(self, group, name, src, dst, device):
        self.count[group] = self.count.get(group, 0) + 1
        pltpu.make_async_remote_copy(
            src_ref=src, dst_ref=dst, send_sem=self.sem(0, group), recv_sem=self.sem(1, name),
            device_id=device, device_id_type=MESH,
        ).start()

    def wait(self, name, ref, device):
        pltpu.make_async_remote_copy(
            src_ref=ref, dst_ref=ref, send_sem=self.sems[0].at[0], recv_sem=self.sem(1, name),
            device_id=device, device_id_type=MESH,
        ).wait_recv()

    def sent(self, group, ref, device):
        pltpu.make_async_remote_copy(
            src_ref=ref, dst_ref=ref, send_sem=self.sem(0, group), recv_sem=self.sems[1].at[0],
            device_id=device, device_id_type=MESH,
        ).wait_send()


def kernel(
    traj_hbm, noise_hbm, shift_hbm, scale_hbm, size, table_hbm, pmap_hbm, wq_hbm, wo_hbm, out,
    traj, noise, shift, scale, table, pmap, wq, stage, shard, slots, perm, w, wt, mod, sizes,
    sum_q, sum_kv, q, k, v, own_t, parts, sums, before, give, full, load, send, recv,
):
    seg, step = lax.axis_index("seg"), lax.axis_index("step")
    x, y, core, z = lax.rem(seg, XN), lax.div(seg, XN), lax.rem(step, 2), lax.div(step, 2)
    other = 1 - core
    net = Net(send, recv)

    def ring(i, n):
        return lax.rem(i + n, n)

    def seg_of(dx, dy):
        return ring(y + dy, YN) * XN + ring(x + dx, XN)

    def at_seg(dx, dy):
        return (seg_of(dx, dy), step)

    def at_z(dz):
        return (seg, ring(z + dz, ZN) * 2 + core)

    sibling = (seg, z * 2 + other)
    following, preceding = (ring(seg + 1, SEGS), step), (ring(seg - 1, SEGS), step)

    peers = [(seg, ring(step + i, STEPS)) for i in range(1, STEPS)]
    peers += [at_seg(i, 0) for i in range(1, XN)] + [at_seg(0, i) for i in (1, -1, 2, -2)] + [following, preceding]
    barrier = pltpu.get_barrier_semaphore()
    for peer in peers:
        pl.semaphore_signal(barrier, inc=1, device_id=peer, device_id_type=MESH)

    near = lax.rem(x, 2)

    def wt_block(dz):
        return wt.at[near, ring(z + dz, ZN), core]

    sources = [
        (wq_hbm, wq), (traj_hbm, traj), (pmap_hbm, pmap), (table_hbm, table), (shift_hbm, shift), (scale_hbm, scale),
        (wo_hbm.at[:, pl.ds(pl.multiple_of(near * HALF, HALF), HALF)], wt_block(0)), (noise_hbm, noise),
    ]
    loads = [pltpu.make_async_copy(src, dst, load.at[i]) for i, (src, dst) in enumerate(sources)]
    for copy in loads:
        copy.start()

    stage[...] = jnp.zeros_like(stage)
    loads[0].wait()
    rows = wq[...].astype(F32)
    for half in range(2):
        for c in range(CHUNKS):
            col = ((c // 3) * 6 + half * 3 + c % 3) * 128
            stage[half, c * SHARD : (c + 1) * SHARD, :] = rows[:, col : col + 128]
    shard[...] = stage[...].astype(BF16)
    slots[step] = shard[core]
    pl.semaphore_wait(barrier, len(peers))

    for dz in (4, 3, 5, 2, 6, 1, 7, 0):
        for swap in range(2):
            if (dz, swap) == (0, 0):
                continue
            there = lax.rem(core + swap, 2)
            net.send("z", "z", shard.at[there], slots.at[step], (seg, ring(z + dz, ZN) * 2 + there))

    mine, low, high = (slice(HALO, HALO + ROWS), slice(HALO, 2 * HALO), slice(ROWS, ROWS + HALO))
    first, last = slice(0, HALO), slice(HALO + ROWS, KEYS)
    for copy in loads[1:]:
        copy.wait()
    onehot = (lax.broadcasted_iota(jnp.int32, (8, ROWS), 0) == pmap[...]).astype(F32)
    chosen = dot(onehot, table[...], ((0,), (0,)), lax.Precision.HIGHEST)
    inputs = traj[0].astype(F32) + chosen
    center = jnp.mean(inputs, axis=-1, keepdims=True)
    inputs = inputs - center
    spread = jnp.mean(jnp.square(inputs), axis=-1, keepdims=True)
    normed = inputs * lax.rsqrt(spread + 1e-06)
    mod[core, mine, :] = (normed * (1.0 + scale[...]) + shift[...]).astype(BF16)
    sizes[core] = jnp.full((8, 128), size[0], F32)
    net.send("mod", "up", mod.at[core, high], mod.at[core, first], following)
    net.send("mod", "down", mod.at[core, low], mod.at[core, last], preceding)
    net.send("mod", "mod", mod.at[core, mine], mod.at[core, mine], sibling)
    net.send("size", "size", sizes.at[core], sizes.at[core], sibling)

    shape = (BLOCK, STEPS * SLOT)
    i = lax.broadcasted_iota(jnp.int32, shape, 0)
    third = lax.shift_right_logical(i * 43, 7)
    j = lax.broadcasted_iota(jnp.int32, shape, 1) - third * SLOT - (i - third * SHARD)
    for c in range(CHUNKS):
        perm[c * BLOCK : (c + 1) * BLOCK, :] = jnp.where(j == c * SHARD, 1.0, 0.0).astype(BF16)
    net.wait("z", slots.at[0 : STEPS - 1], sibling)
    block = dot(perm[...], slots[...].reshape(STEPS * SLOT, 128)).astype(BF16)

    ours = 1 + lax.rem(z, 2)

    def part(which, dx, dy):
        return w.at[which, pl.ds(pl.multiple_of(seg_of(dx, dy) * BLOCK, BLOCK), BLOCK)]

    def blocks(n):
        return w.at[:, 0 : n * BLOCK // 3]

    for c in range(CHUNKS):
        own_rows = pl.ds(pl.multiple_of(seg * BLOCK, BLOCK), BLOCK)
        w[c // 3, own_rows, (c % 3) * 128 : (c % 3 + 1) * 128] = block[c * BLOCK : (c + 1) * BLOCK]

    def pass_on(name, ref, device):
        net.send("w", name, ref, ref, device)

    top = YN // 2

    def goes(way, far, is_b, dx=0):
        return far < top or (way == 1) == (is_b or dx % 2 == 0)

    def send_ax(way):
        pass_on(("ax", -way % XN), part(ours, 0, 0), at_seg(way, 0))

    def wait_ax(dx):
        net.wait(("ax", dx % XN), part(ours, dx, 0), sibling)

    def send_ay(dx, way, far):
        ref = part(ours, dx, -way * far)
        if far + 1 < top:
            pass_on(("ay", dx, way, far + 1), ref, at_seg(0, way))
        if far + 2 == top and goes(way, top, False, dx):
            pass_on(("ay", dx, way, top), ref, at_seg(0, 2 * way))

    def wait_ay(dx, way, far):
        net.wait(("ay", dx, way, far), part(ours, dx, -way * far), sibling)

    def send_az(dx, dy):
        pass_on(("az", abs(dy)), part(ours, dx, dy), at_z(1 if dx % 2 == 0 else -1))

    def send_by(way, far):
        ref = part(0, 0, -way * far)
        if far + 1 < top:
            pass_on(("by", way, far + 1), ref, at_seg(0, way))
        if far + 2 == top and goes(way, top, True):
            pass_on(("by", way, top), ref, at_seg(0, 2 * way))

    def wait_by(way, far):
        net.wait(("by", way, far), part(0, 0, -way * far), sibling)

    def relayed(far):
        return far < top - 1

    def send_bx(way_y, far):
        dy = -way_y * far
        relay = way_y if relayed(far) else 0
        for way in (1, -1):
            pass_on(("bxr", dy) if way == relay else ("bx", far), part(0, 0, dy), at_seg(way, 0))
        if not relay:
            pass_on(("bx", far), part(0, 0, dy), at_seg(2, 0))

    def relay_bx(way_y, far):
        dy = -way_y * far
        net.wait(("bxr", dy), part(0, -way_y, dy), sibling)
        pass_on(("bx", far), part(0, -way_y, dy), at_seg(way_y, 0))

    def settle(far):
        both = 2 if 0 < far < top else 1
        net.wait(("bx", far), blocks(both * (2 if relayed(far) else 3)), sibling)
        net.wait(("az", far), blocks(both * XN - (far == 0)), sibling)

    def send_wz(way, far):
        if far + 1 < ZN // 2 or (far + 1 == ZN // 2 and way == 1):
            net.send("wz", ("wz", way, far + 1), wt_block(-way * far), wt_block(-way * far), at_z(way))

    def take_wz(way, far):
        net.wait(("wz", way, far), wt_block(-way * far), sibling)
        send_wz(way, far)

    def project(pair, start):
        rows = pl.ds(pl.multiple_of(pair * PAIR, PAIR), PAIR)
        everyone = mod[:, :, rows].reshape(2 * KEYS, PAIR)
        asked = mod[:, mine, rows].reshape(2 * ROWS, PAIR)
        add_q, add_k, add_v = dot(asked, w[0, rows]), dot(everyone, w[1, rows]), dot(everyone, w[2, rows])
        sum_q[...] = add_q if start else sum_q[...] + add_q
        sum_kv[0] = add_k if start else sum_kv[0] + add_k
        sum_kv[1] = add_v if start else sum_kv[1] + add_v

    send_ax(1)
    send_ax(-1)
    send_ay(0, 1, 0)
    send_ay(0, -1, 0)
    pass_on(("ax", 2), part(ours, 0, 0), at_seg(2, 0))
    send_by(1, 0)
    send_by(-1, 0)
    send_bx(1, 0)
    send_wz(1, 0)
    send_wz(-1, 0)
    for dx in (3, 1, 2):
        wait_ax(dx)
        send_ay(dx, 1, 0)
        send_ay(dx, -1, 0)
        send_az(dx, 0)
    net.wait("up", mod.at[core, first], sibling)
    net.send("mod", "mod", mod.at[core, first], mod.at[core, first], sibling)
    net.wait("down", mod.at[core, last], sibling)
    net.send("mod", "mod", mod.at[core, last], mod.at[core, last], sibling)

    pair = lax.div(y, 2)
    side = 1 - 2 * lax.rem(y, 2)
    pairs = [pair, ring(pair - side, YN // 2), ring(pair + side, YN // 2), ring(pair + 2, YN // 2)]

    for far in range(1, top + 1):
        for way in (1, -1):
            if goes(way, far, True):
                wait_by(way, far)
                send_by(way, far)
                send_bx(way, far)
        for way in (1, -1):
            if relayed(far - 1) and (far > 1 or way == 1):
                relay_bx(way, far - 1)
        for dx in (0, 3, 1, 2):
            for way in (1, -1):
                if goes(way, far, False, dx):
                    wait_ay(dx, way, far)
                    send_ay(dx, way, far)
                    send_az(dx, -way * far)
        for way in (1, -1):
            if far < top or way == 1:
                take_wz(way, far)
        if far == 1:
            settle(0)
        elif far < top:
            if far == 2:
                net.wait("mod", mod.at[other], sibling)
                net.wait("size", sizes.at[other], sibling)
            settle(far - 1)
            project(pairs[far - 2], far == 2)

    for way, zs in ((1, slice(0, ZN // 2)), (-1, slice(ZN // 2, ZN))):
        net.send("wx", "wx", wt.at[near, zs, core], wt.at[near, zs, core], at_seg(way, 0))
    net.send("ws", "ws", wt.at[near, :, core], wt.at[near, :, core], sibling)
    settle(top - 1)
    project(pairs[2], False)
    settle(top)
    project(pairs[3], False)
    for c in range(3):
        cols = slice(c * 128, (c + 1) * 128)
        q[c] = (sum_q[:, cols].astype(BF16) * 0.125).astype(BF16).reshape(2, ROWS, 128)
        k[c] = sum_kv[0, :, cols].astype(BF16).reshape(2, KEYS, 128)
        v[c] = sum_kv[1, :, cols].astype(BF16).reshape(2, KEYS, 128)

    at_q = lax.broadcasted_iota(jnp.int32, (ROWS, KEYS), 0)
    at_k = lax.broadcasted_iota(jnp.int32, (ROWS, KEYS), 1)
    frame = seg * ROWS - HALO + at_k
    allowed = (at_k >= at_q) & (at_k <= at_q + 2 * HALO) & (frame >= 0) & (frame < SEGS * ROWS)
    bias = jnp.where(allowed, 0.0, -1e30).astype(F32)
    bias = jnp.concatenate([bias, bias], axis=0)
    lane = lax.broadcasted_iota(jnp.int32, (ROWS, 128), 1)
    ones = jnp.ones((KEYS, 128), BF16)
    for c in range(3):
        total = None
        for s in range(2):
            asked = q[c, s]
            nothing = jnp.zeros_like(asked)
            both = jnp.concatenate([jnp.where(lane < 64, asked, nothing), jnp.where(lane < 64, nothing, asked)], axis=0)
            scores = dot(both, k[c, s], ((1,), (1,))) + bias
            lifted = jnp.exp(scores - jnp.max(scores, axis=1, keepdims=True)).astype(BF16)
            got = dot(lifted, v[c, s]) / dot(lifted, ones)
            got = jnp.where(lane < 64, got[:ROWS], got[ROWS:]).astype(BF16)
            term = got.astype(F32) * sizes[s, 0:1, :]
            if s == 0:
                own_t[:, c * 128 : (c + 1) * 128] = term.astype(BF16)
                total = term
            else:
                total = total + term
        give[:, c * 128 : (c + 1) * 128] = total.astype(BF16)

    share = ROWS // ZN

    def share_rows(i):
        return pl.ds(pl.multiple_of(i * share, share), share)

    for dz in (4, 3, 5, 2, 6, 1, 7):
        net.send("there", "there", give.at[share_rows(ring(z + dz, ZN))], parts.at[z], at_z(dz))
    parts[z] = give[share_rows(z), :]
    net.wait("wx", wt.at[1 - near, :, core], sibling)
    net.send("ws", "ws", wt.at[1 - near, :, core], wt.at[1 - near, :, core], sibling)
    net.wait("there", parts.at[0 : ZN - 1], sibling)
    total = jnp.zeros((share, HALF), F32)
    for i in range(ZN):
        sums[i] = total.astype(BF16)
        total = total + parts[i].astype(F32)
    for dz in (4, 3, 5, 2, 6, 1, 7):
        net.send("back", "back", sums.at[ring(z + dz, ZN)], before.at[share_rows(z)], at_z(dz))
    before[share_rows(z), :] = sums[z]
    net.wait("ws", wt.at[:, :, other], sibling)
    net.wait("back", before.at[0 : ROWS - share], sibling)

    even = before[...]
    odd = (even.astype(F32) + own_t[...].astype(F32)).astype(BF16)
    full[core] = jnp.where(core == 0, even, odd)
    own_t[...] = jnp.where(core == 0, odd, even)
    net.send("full", "full", own_t, full.at[core], sibling)
    drift = dot(full[core], wt[core].reshape(D, HALF), ((1,), (1,)))
    net.wait("full", full.at[other], sibling)
    drift = drift + dot(full[other], wt[other].reshape(D, HALF), ((1,), (1,)))
    out[...] = (noise[...].astype(F32) + drift).astype(BF16)

    net.sent("z", slots.at[0 : STEPS - 1], sibling)
    net.sent("mod", mod.at[:, 0 : HALO + ROWS], sibling)
    net.sent("size", sizes.at[0], sibling)
    net.sent("w", blocks(net.count["w"]), sibling)
    net.sent("wz", wt.at[0, 0 : ZN - 1, 0], sibling)
    net.sent("wx", wt.at[0, :, 0], sibling)
    net.sent("ws", wt.at[:, :, 0], sibling)
    net.sent("there", parts.at[0 : ZN - 1], sibling)
    net.sent("back", parts.at[0 : ZN - 1], sibling)
    net.sent("full", own_t, sibling)


def shards(trajectory, noise, mod_shift, mod_scale, step_size, prompt_table, prompt_map, w_qkv, w_out):
    vmem = pl.BlockSpec(memory_space=pltpu.VMEM)
    smem = pl.BlockSpec(memory_space=pltpu.SMEM)
    hbm = pl.BlockSpec(memory_space=pl.ANY)
    result = pl.pallas_call(
        kernel,
        out_shape=jax.ShapeDtypeStruct((ROWS, D), BF16),
        in_specs=[hbm, hbm, hbm, hbm, smem, hbm, hbm, hbm, hbm],
        out_specs=vmem,
        scratch_shapes=[
            pltpu.VMEM((1, ROWS, D), BF16),
            pltpu.VMEM((ROWS, D), BF16),
            pltpu.VMEM((1, D), F32),
            pltpu.VMEM((1, D), F32),
            pltpu.VMEM((8, D), F32),
            pltpu.VMEM((1, ROWS), jnp.int32),
            pltpu.VMEM((SHARD, 3 * HQ), BF16),
            pltpu.VMEM((2, SLOT, 128), F32),
            pltpu.VMEM((2, SLOT, 128), BF16),
            pltpu.VMEM((STEPS, SLOT, 128), BF16),
            pltpu.VMEM((CHUNKS * BLOCK, STEPS * SLOT), BF16),
            pltpu.VMEM((3, D, HALF), BF16),
            pltpu.VMEM((2, ZN, 2, WO, HALF), BF16),
            pltpu.VMEM((2, KEYS, D), BF16),
            pltpu.VMEM((2, 8, 128), F32),
            pltpu.VMEM((2 * ROWS, HALF), F32),
            pltpu.VMEM((2, 2 * KEYS, HALF), F32),
            pltpu.VMEM((3, 2, ROWS, 128), BF16),
            pltpu.VMEM((3, 2, KEYS, 128), BF16),
            pltpu.VMEM((3, 2, KEYS, 128), BF16),
            pltpu.VMEM((ROWS, HALF), BF16),
            pltpu.VMEM((ZN, ROWS // ZN, HALF), BF16),
            pltpu.VMEM((ZN, ROWS // ZN, HALF), BF16),
            pltpu.VMEM((ROWS, HALF), BF16),
            pltpu.VMEM((ROWS, HALF), BF16),
            pltpu.VMEM((2, ROWS, HALF), BF16),
            pltpu.SemaphoreType.DMA((8,)),
            pltpu.SemaphoreType.DMA((SENDS,)),
            pltpu.SemaphoreType.DMA((RECVS,)),
        ],
        compiler_params=pltpu.CompilerParams(
            collective_id=0, has_side_effects=True, vmem_limit_bytes=60 * 1024 * 1024
        ),
    )(
        trajectory, noise, mod_shift, mod_scale, step_size, prompt_table,
        prompt_map.reshape(1, ROWS), w_qkv, w_out.T,
    )
    return result[None]


def solution(mesh):
    return jax.shard_map(
        shards,
        mesh=mesh,
        in_specs=(
            P("step", "seg", None),
            P("seg", None),
            P("step", None),
            P("step", None),
            P("step"),
            P(),
            P("seg"),
            P(("seg", "step"), None),
            P(None, "step"),
        ),
        out_specs=P("step", "seg", None),
        check_vma=False,
    )
```

time: 79.7 us -> 65.7 us (0.82)
  Pallas kernels: 77.1 us -> 63.1 us
    pallas_call x1, Pallas kernels: 77.1 us -> 63.1 us  [shards(): pl.pallas_call(kernel, out_shape=jax.ShapeDtypeStruct((ROWS, D), BF16), i...]
where the time goes in v3:
time: 65.7 us; the launch traced here: 65.5 us
  Pallas kernels  63.1 us (96%)
  local copies, waits for them, and re-layouts  1.77 us (3%)
  between operations  0.66 us (1%)
    pallas_call x1, Pallas kernels, shards(): pl.pallas_call(kernel, out_shape=jax.ShapeDtypeStruct((ROWS, D), BF16), i...  63.1 us
    unnamed x1, local copies, waits for them, and re-layouts  1.77 us

profile of v3, /device:TPU:1, one launch (start us, length us, event | category | flops | bytes accessed | tf_op | source)
XLA Modules:
  0.0 65.5 jit_solution(3820738750311047106)
XLA Ops:
  0.7 63.1 %shard_map.91 = bf16[128,1536]{1,0:T(8,128)(2,1)} custom-call(bf16[1,128,1536]{2,1,0:T(8,128)(2,1)} %traj_hbm.1, bf16[128,1536]{1,0:T(8,128)(2,1)} %noise_hbm.1, f32[1,1536]{1,0:T(1,128)} %shift_hbm.1, f32[1,1536]{1,0:T(1,128)} %scale_hbm.1, f32[1]{0:T(128)S(6)} %copy.11.size, f32[8,1536]{1,0:T(8,128)} %table_hbm.1, s32[1,128]{1,0:T(1,128)} %bitcast.5, ...), custom_call_target="tpu_custom_call" | custom-call | tf_op jit(solution)/shard_map/pallas_call | solution.py:372
  63.7 1.8 %copy.12 = bf16[1,128,1536]{2,1,0:T(8,128)(2,1)} copy(bf16[1,128,1536]{2,1,0:T(8,128)(2,1)} %bitcast.3) | data formatting | bytes 786432

commit v4 on v3

--- a/solution.py
+++ b/solution.py
@@ -59,7 +59,7 @@
 def kernel(
     traj_hbm, noise_hbm, shift_hbm, scale_hbm, size, table_hbm, pmap_hbm, wq_hbm, wo_hbm, out,
     traj, noise, shift, scale, table, pmap, wq, stage, shard, slots, perm, w, wt, mod, sizes,
-    sum_q, sum_kv, q, k, v, own_t, parts, sums, before, give, full, load, send, recv,
+    sum_q, sum_kv, q, k, v, own_t, parts, sums, before, give, full, extra, start, load, send, recv,
 ):
     seg, step = lax.axis_index("seg"), lax.axis_index("step")
     x, y, core, z = lax.rem(seg, XN), lax.div(seg, XN), lax.rem(step, 2), lax.div(step, 2)
@@ -82,7 +82,8 @@
     following, preceding = (ring(seg + 1, SEGS), step), (ring(seg - 1, SEGS), step)
 
     peers = [(seg, ring(step + i, STEPS)) for i in range(1, STEPS)]
-    peers += [at_seg(i, 0) for i in range(1, XN)] + [at_seg(0, i) for i in (1, -1, 2, -2)] + [following, preceding]
+    peers += [at_seg(i, j) for i in range(XN) for j in (0, 1, -1) if (i, j) != (0, 0)]
+    peers += [at_seg(0, 2), at_seg(0, -2), following, preceding]
     barrier = pltpu.get_barrier_semaphore()
     for peer in peers:
         pl.semaphore_signal(barrier, inc=1, device_id=peer, device_id_type=MESH)
@@ -122,8 +123,14 @@
     first, last = slice(0, HALO), slice(HALO + ROWS, KEYS)
     for copy in loads[1:]:
         copy.wait()
+    whole = table[...]
+    upper = whole.astype(BF16)
+    rest = whole - upper.astype(F32)
+    middle = rest.astype(BF16)
+    lower = (rest - middle.astype(F32)).astype(BF16)
     onehot = (lax.broadcasted_iota(jnp.int32, (8, ROWS), 0) == pmap[...]).astype(F32)
-    chosen = dot(onehot, table[...], ((0,), (0,)), lax.Precision.HIGHEST)
+    onehot = jnp.concatenate([onehot, onehot, onehot], axis=0).astype(BF16)
+    chosen = dot(onehot, jnp.concatenate([upper, middle, lower], axis=0), ((0,), (0,)))
     inputs = traj[0].astype(F32) + chosen
     center = jnp.mean(inputs, axis=-1, keepdims=True)
     inputs = inputs - center
@@ -165,8 +172,9 @@
     def goes(way, far, is_b, dx=0):
         return far < top or (way == 1) == (is_b or dx % 2 == 0)
 
-    def send_ax(way):
-        pass_on(("ax", -way % XN), part(ours, 0, 0), at_seg(way, 0))
+    def send_a(dx, way):
+        name = ("ay", -dx % XN, way, 1) if way else ("ax", -dx % XN)
+        pass_on(name, part(ours, 0, 0), at_seg(dx, way))
 
     def wait_ax(dx):
         net.wait(("ax", dx % XN), part(ours, dx, 0), sibling)
@@ -184,12 +192,9 @@
     def send_az(dx, dy):
         pass_on(("az", abs(dy)), part(ours, dx, dy), at_z(1 if dx % 2 == 0 else -1))
 
-    def send_by(way, far):
-        ref = part(0, 0, -way * far)
-        if far + 1 < top:
-            pass_on(("by", way, far + 1), ref, at_seg(0, way))
-        if far + 2 == top and goes(way, top, True):
-            pass_on(("by", way, top), ref, at_seg(0, 2 * way))
+    def send_by(way, far, hops):
+        if far + hops < top or goes(way, top, True):
+            pass_on(("by", way, far + hops), part(0, 0, -way * far), at_seg(0, hops * way))
 
     def wait_by(way, far):
         net.wait(("by", way, far), part(0, 0, -way * far), sibling)
@@ -232,56 +237,74 @@
         sum_kv[0] = add_k if start else sum_kv[0] + add_k
         sum_kv[1] = add_v if start else sum_kv[1] + add_v
 
-    send_ax(1)
-    send_ax(-1)
-    send_ay(0, 1, 0)
-    send_ay(0, -1, 0)
-    pass_on(("ax", 2), part(ours, 0, 0), at_seg(2, 0))
-    send_by(1, 0)
-    send_by(-1, 0)
+    for dx in (0, 1, 3, 2):
+        send_a(dx, 1)
+        send_a(dx, -1)
+    for hops in (1, 2):
+        send_by(1, 0, hops)
+        send_by(-1, 0, hops)
+    for dx in (1, 3, 2):
+        send_a(dx, 0)
     send_bx(1, 0)
     send_wz(1, 0)
     send_wz(-1, 0)
+
+    pair = lax.div(y, 2)
+    side = 1 - 2 * lax.rem(y, 2)
+    pairs = [pair, ring(pair - side, YN // 2), ring(pair + side, YN // 2), ring(pair + 2, YN // 2)]
+
+    def take_ay(fars):
+        for far in fars:
+            for dx in (0, 3, 1, 2):
+                for way in (1, -1):
+                    if goes(way, far, False, dx):
+                        wait_ay(dx, way, far)
+                        send_ay(dx, way, far)
+                        send_az(dx, -way * far)
+
+    def take_by(fars):
+        for far in fars:
+            for way in (1, -1):
+                if goes(way, far, True):
+                    wait_by(way, far)
+                    if far == 2:
+                        send_by(way, far, 1)
+                        send_by(way, far, 2)
+                    send_bx(way, far)
+
+    take_ay((1,))
+    take_by((1, 2))
     for dx in (3, 1, 2):
         wait_ax(dx)
-        send_ay(dx, 1, 0)
-        send_ay(dx, -1, 0)
         send_az(dx, 0)
+    relay_bx(1, 0)
     net.wait("up", mod.at[core, first], sibling)
     net.send("mod", "mod", mod.at[core, first], mod.at[core, first], sibling)
     net.wait("down", mod.at[core, last], sibling)
     net.send("mod", "mod", mod.at[core, last], mod.at[core, last], sibling)
-
-    pair = lax.div(y, 2)
-    side = 1 - 2 * lax.rem(y, 2)
-    pairs = [pair, ring(pair - side, YN // 2), ring(pair + side, YN // 2), ring(pair + 2, YN // 2)]
-
-    for far in range(1, top + 1):
-        for way in (1, -1):
-            if goes(way, far, True):
-                wait_by(way, far)
-                send_by(way, far)
-                send_bx(way, far)
-        for way in (1, -1):
-            if relayed(far - 1) and (far > 1 or way == 1):
-                relay_bx(way, far - 1)
-        for dx in (0, 3, 1, 2):
-            for way in (1, -1):
-                if goes(way, far, False, dx):
-                    wait_ay(dx, way, far)
-                    send_ay(dx, way, far)
-                    send_az(dx, -way * far)
-        for way in (1, -1):
-            if far < top or way == 1:
-                take_wz(way, far)
-        if far == 1:
-            settle(0)
-        elif far < top:
-            if far == 2:
-                net.wait("mod", mod.at[other], sibling)
-                net.wait("size", sizes.at[other], sibling)
-            settle(far - 1)
-            project(pairs[far - 2], far == 2)
+    take_wz(1, 1)
+    take_wz(-1, 1)
+
+    take_ay((2,))
+    relay_bx(1, 1)
+    relay_bx(-1, 1)
+    take_by((3, 4))
+    relay_bx(1, 2)
+    relay_bx(-1, 2)
+    settle(0)
+    net.wait("mod", mod.at[other], sibling)
+    net.wait("size", sizes.at[other], sibling)
+    take_wz(1, 2)
+    take_wz(-1, 2)
+
+    take_ay((3, 4))
+    settle(1)
+    project(pairs[0], True)
+    take_wz(1, 3)
+    take_wz(-1, 3)
+    settle(2)
+    project(pairs[1], False)
+    take_wz(1, 4)
 
     for way, zs in ((1, slice(0, ZN // 2)), (-1, slice(ZN // 2, ZN))):
         net.send("wx", "wx", wt.at[near, zs, core], wt.at[near, zs, core], at_seg(way, 0))
@@ -327,6 +350,7 @@
     def share_rows(i):
         return pl.ds(pl.multiple_of(i * share, share), share)
 
+    net.send("own", "own", own_t, extra.at[core], sibling)
     for dz in (4, 3, 5, 2, 6, 1, 7):
         net.send("there", "there", give.at[share_rows(ring(z + dz, ZN))], parts.at[z], at_z(dz))
     parts[z] = give[share_rows(z), :]
@@ -341,17 +365,17 @@
         net.send("back", "back", sums.at[ring(z + dz, ZN)], before.at[share_rows(z)], at_z(dz))
     before[share_rows(z), :] = sums[z]
     net.wait("ws", wt.at[:, :, other], sibling)
+    net.wait("own", extra.at[other], sibling)
+    odd = jnp.where(core == 0, jnp.zeros((ROWS, HALF), BF16), extra[other])
+    base = dot(odd, wt[other].reshape(D, HALF), ((1,), (1,)))
+    odd = jnp.where(core == 0, jnp.zeros((ROWS, HALF), BF16), own_t[...])
+    start[...] = noise[...].astype(F32) + base + dot(odd, wt[core].reshape(D, HALF), ((1,), (1,)))
     net.wait("back", before.at[0 : ROWS - share], sibling)
 
-    even = before[...]
-    odd = (even.astype(F32) + own_t[...].astype(F32)).astype(BF16)
-    full[core] = jnp.where(core == 0, even, odd)
-    own_t[...] = jnp.where(core == 0, odd, even)
-    net.send("full", "full", own_t, full.at[core], sibling)
-    drift = dot(full[core], wt[core].reshape(D, HALF), ((1,), (1,)))
+    net.send("full", "full", before, full.at[core], sibling)
+    start[...] += dot(before[...], wt[core].reshape(D, HALF), ((1,), (1,)))
     net.wait("full", full.at[other], sibling)
-    drift = drift + dot(full[other], wt[other].reshape(D, HALF), ((1,), (1,)))
-    out[...] = (noise[...].astype(F32) + drift).astype(BF16)
+    out[...] = (start[...] + dot(full[other], wt[other].reshape(D, HALF), ((1,), (1,)))).astype(BF16)
 
     net.sent("z", slots.at[0 : STEPS - 1], sibling)
     net.sent("mod", mod.at[:, 0 : HALO + ROWS], sibling)
@@ -362,7 +386,8 @@
     net.sent("ws", wt.at[:, :, 0], sibling)
     net.sent("there", parts.at[0 : ZN - 1], sibling)
     net.sent("back", parts.at[0 : ZN - 1], sibling)
-    net.sent("full", own_t, sibling)
+    net.sent("own", own_t, sibling)
+    net.sent("full", before, sibling)
 
 
 def shards(trajectory, noise, mod_shift, mod_scale, step_size, prompt_table, prompt_map, w_qkv, w_out):
@@ -401,6 +426,8 @@
             pltpu.VMEM((ROWS, HALF), BF16),
             pltpu.VMEM((ROWS, HALF), BF16),
             pltpu.VMEM((2, ROWS, HALF), BF16),
+            pltpu.VMEM((2, ROWS, HALF), BF16),
+            pltpu.VMEM((ROWS, D), F32),
             pltpu.SemaphoreType.DMA((8,)),
             pltpu.SemaphoreType.DMA((SENDS,)),
             pltpu.SemaphoreType.DMA((RECVS,)),

time: 65.7 us -> 63.9 us (0.973)
  Pallas kernels: 63.1 us -> 61.3 us
    pallas_call x1, Pallas kernels: 63.1 us -> 61.3 us  [shards(): pl.pallas_call(kernel, out_shape=jax.ShapeDtypeStruct((ROWS, D), BF16), i...]
where the time goes in v4:
time: 63.9 us; the launch traced here: 63.7 us
  Pallas kernels  61.3 us (96%)
  local copies, waits for them, and re-layouts  1.77 us (3%)
  between operations  0.66 us (1%)
    pallas_call x1, Pallas kernels, shards(): pl.pallas_call(kernel, out_shape=jax.ShapeDtypeStruct((ROWS, D), BF16), i...  61.3 us
    unnamed x1, local copies, waits for them, and re-layouts  1.77 us

profile of v4, /device:TPU:1, one launch (start us, length us, event | category | flops | bytes accessed | tf_op | source)
XLA Modules:
  0.0 63.7 jit_solution(14850136157232723800)
XLA Ops:
  0.7 61.3 %shard_map.91 = bf16[128,1536]{1,0:T(8,128)(2,1)} custom-call(bf16[1,128,1536]{2,1,0:T(8,128)(2,1)} %traj_hbm.1, bf16[128,1536]{1,0:T(8,128)(2,1)} %noise_hbm.1, f32[1,1536]{1,0:T(1,128)} %shift_hbm.1, f32[1,1536]{1,0:T(1,128)} %scale_hbm.1, f32[1]{0:T(128)S(6)} %copy.11.size, f32[8,1536]{1,0:T(8,128)} %table_hbm.1, s32[1,128]{1,0:T(1,128)} %bitcast.5, ...), custom_call_target="tpu_custom_call" | custom-call | tf_op jit(solution)/shard_map/pallas_call | solution.py:397
  61.9 1.8 %copy.12 = bf16[1,128,1536]{2,1,0:T(8,128)(2,1)} copy(bf16[1,128,1536]{2,1,0:T(8,128)(2,1)} %bitcast.3) | data formatting | bytes 786432

commit v5 on v4

--- a/solution.py
+++ b/solution.py
@@ -21,7 +21,7 @@
 SLOT = 32
 WO = D // STEPS
 PAIR = 2 * XN * BLOCK
-SENDS, RECVS = 12, 80
+SENDS, RECVS = 11, 85
 
 
 def dot(a, b, contract=((1,), (0,)), precision=None):
@@ -82,8 +82,7 @@
     following, preceding = (ring(seg + 1, SEGS), step), (ring(seg - 1, SEGS), step)
 
     peers = [(seg, ring(step + i, STEPS)) for i in range(1, STEPS)]
-    peers += [at_seg(i, j) for i in range(XN) for j in (0, 1, -1) if (i, j) != (0, 0)]
-    peers += [at_seg(0, 2), at_seg(0, -2), following, preceding]
+    peers += [at_seg(i, 0) for i in range(1, XN)] + [at_seg(0, i) for i in (1, -1, 2, -2)] + [following, preceding]
     barrier = pltpu.get_barrier_semaphore()
     for peer in peers:
         pl.semaphore_signal(barrier, inc=1, device_id=peer, device_id_type=MESH)
@@ -119,10 +118,20 @@
             there = lax.rem(core + swap, 2)
             net.send("z", "z", shard.at[there], slots.at[step], (seg, ring(z + dz, ZN) * 2 + there))
 
+    def send_wz(way, far):
+        if far + 1 < ZN // 2 or (far + 1 == ZN // 2 and way == 1):
+            net.send("wz", ("wz", way, far + 1), wt_block(-way * far), wt_block(-way * far), at_z(way))
+
+    def take_wz(way, far):
+        net.wait(("wz", way, far), wt_block(-way * far), sibling)
+        send_wz(way, far)
+
     mine, low, high = (slice(HALO, HALO + ROWS), slice(HALO, 2 * HALO), slice(ROWS, ROWS + HALO))
     first, last = slice(0, HALO), slice(HALO + ROWS, KEYS)
     for copy in loads[1:]:
         copy.wait()
+    send_wz(1, 0)
+    send_wz(-1, 0)
     whole = table[...]
     upper = whole.astype(BF16)
     rest = whole - upper.astype(F32)
@@ -172,61 +181,64 @@
     def goes(way, far, is_b, dx=0):
         return far < top or (way == 1) == (is_b or dx % 2 == 0)
 
-    def send_a(dx, way):
-        name = ("ay", -dx % XN, way, 1) if way else ("ax", -dx % XN)
-        pass_on(name, part(ours, 0, 0), at_seg(dx, way))
-
-    def wait_ax(dx):
-        net.wait(("ax", dx % XN), part(ours, dx, 0), sibling)
+    def send_ax(dx):
+        pass_on(("ax", -dx % XN), part(0, 0, 0), at_seg(dx, 0))
+
+    def take_ax(dx):
+        net.wait(("ax", dx % XN), part(0, dx, 0), sibling)
+        send_ay(dx, 1, 0)
+        send_ay(dx, -1, 0)
 
     def send_ay(dx, way, far):
-        ref = part(ours, dx, -way * far)
+        ref = part(0, dx, -way * far)
         if far + 1 < top:
             pass_on(("ay", dx, way, far + 1), ref, at_seg(0, way))
         if far + 2 == top and goes(way, top, False, dx):
             pass_on(("ay", dx, way, top), ref, at_seg(0, 2 * way))
 
-    def wait_ay(dx, way, far):
-        net.wait(("ay", dx, way, far), part(ours, dx, -way * far), sibling)
+    def take_ay(dx, far):
+        for way in (1, -1):
+            if goes(way, far, False, dx):
+                net.wait(("ay", dx, way, far), part(0, dx, -way * far), sibling)
+                send_ay(dx, way, far)
 
     def send_az(dx, dy):
         pass_on(("az", abs(dy)), part(ours, dx, dy), at_z(1 if dx % 2 == 0 else -1))
 
     def send_by(way, far, hops):
         if far + hops < top or goes(way, top, True):
-            pass_on(("by", way, far + hops), part(0, 0, -way * far), at_seg(0, hops * way))
-
-    def wait_by(way, far):
-        net.wait(("by", way, far), part(0, 0, -way * far), sibling)
+            pass_on(("by", way, far + hops), part(ours, 0, -way * far), at_seg(0, hops * way))
+
+    def take_by(far):
+        for way in (1, -1):
+            if goes(way, far, True):
+                net.wait(("by", way, far), part(ours, 0, -way * far), sibling)
+                if far == 2:
+                    send_by(way, far, 1)
+                    send_by(way, far, 2)
+                send_bx(way, far)
+                send_az(0, -way * far)
 
     def relayed(far):
-        return far < top - 1
-
-    def send_bx(way_y, far):
-        dy = -way_y * far
-        relay = way_y if relayed(far) else 0
+        return 0 < far < top - 1
+
+    def send_bx(way, far):
+        for dx in (1, -1) if relayed(far) else (2, 1, -1):
+            pass_on(("bx", -way * far, -dx % XN), part(ours, 0, -way * far), at_seg(dx, 0))
+
+    def take_bx(far, opposite):
         for way in (1, -1):
-            pass_on(("bxr", dy) if way == relay else ("bx", far), part(0, 0, dy), at_seg(way, 0))
-        if not relay:
-            pass_on(("bx", far), part(0, 0, dy), at_seg(2, 0))
-
-    def relay_bx(way_y, far):
-        dy = -way_y * far
-        net.wait(("bxr", dy), part(0, -way_y, dy), sibling)
-        pass_on(("bx", far), part(0, -way_y, dy), at_seg(way_y, 0))
+            if not goes(way, far, True) or (far == 0 and way == -1):
+                continue
+            for dx in (2,) if opposite else (-way, way):
+                ref = part(ours, dx, -way * far)
+                net.wait(("bx", -way * far, dx % XN), ref, sibling)
+                if relayed(far) and dx == -way:
+                    pass_on(("bx", -way * far, 2), ref, at_seg(way, 0))
+                send_az(dx, -way * far)
 
     def settle(far):
-        both = 2 if 0 < far < top else 1
-        net.wait(("bx", far), blocks(both * (2 if relayed(far) else 3)), sibling)
-        net.wait(("az", far), blocks(both * XN - (far == 0)), sibling)
-
-    def send_wz(way, far):
-        if far + 1 < ZN // 2 or (far + 1 == ZN // 2 and way == 1):
-            net.send("wz", ("wz", way, far + 1), wt_block(-way * far), wt_block(-way * far), at_z(way))
-
-    def take_wz(way, far):
-        net.wait(("wz", way, far), wt_block(-way * far), sibling)
-        send_wz(way, far)
+        net.wait(("az", far), blocks((2 if 0 < far < top else 1) * XN - (far == 0)), sibling)
 
     def project(pair, start):
         rows = pl.ds(pl.multiple_of(pair * PAIR, PAIR), PAIR)
@@ -237,74 +249,60 @@
         sum_kv[0] = add_k if start else sum_kv[0] + add_k
         sum_kv[1] = add_v if start else sum_kv[1] + add_v
 
-    for dx in (0, 1, 3, 2):
-        send_a(dx, 1)
-        send_a(dx, -1)
+    for dx in (1, -1, 2):
+        send_ax(dx)
     for hops in (1, 2):
         send_by(1, 0, hops)
         send_by(-1, 0, hops)
-    for dx in (1, 3, 2):
-        send_a(dx, 0)
+    send_ay(0, 1, 0)
+    send_ay(0, -1, 0)
     send_bx(1, 0)
-    send_wz(1, 0)
-    send_wz(-1, 0)
+    take_wz(1, 1)
+    take_wz(-1, 1)
 
     pair = lax.div(y, 2)
     side = 1 - 2 * lax.rem(y, 2)
     pairs = [pair, ring(pair - side, YN // 2), ring(pair + side, YN // 2), ring(pair + 2, YN // 2)]
 
-    def take_ay(fars):
-        for far in fars:
-            for dx in (0, 3, 1, 2):
-                for way in (1, -1):
-                    if goes(way, far, False, dx):
-                        wait_ay(dx, way, far)
-                        send_ay(dx, way, far)
-                        send_az(dx, -way * far)
-
-    def take_by(fars):
-        for far in fars:
-            for way in (1, -1):
-                if goes(way, far, True):
-                    wait_by(way, far)
-                    if far == 2:
-                        send_by(way, far, 1)
-                        send_by(way, far, 2)
-                    send_bx(way, far)
-
-    take_ay((1,))
-    take_by((1, 2))
     for dx in (3, 1, 2):
-        wait_ax(dx)
-        send_az(dx, 0)
-    relay_bx(1, 0)
+        take_ax(dx)
+    take_by(1)
+    take_by(2)
+    take_ay(0, 1)
+    take_bx(0, False)
     net.wait("up", mod.at[core, first], sibling)
     net.send("mod", "mod", mod.at[core, first], mod.at[core, first], sibling)
     net.wait("down", mod.at[core, last], sibling)
     net.send("mod", "mod", mod.at[core, last], mod.at[core, last], sibling)
-    take_wz(1, 1)
-    take_wz(-1, 1)
-
-    take_ay((2,))
-    relay_bx(1, 1)
-    relay_bx(-1, 1)
-    take_by((3, 4))
-    relay_bx(1, 2)
-    relay_bx(-1, 2)
-    settle(0)
+    take_wz(1, 2)
+    take_wz(-1, 2)
+    for dx in (3, 1, 2):
+        take_ay(dx, 1)
+    take_bx(1, False)
+    take_bx(2, False)
+    take_bx(0, True)
+    take_by(3)
+    take_by(4)
+    take_wz(1, 3)
+    take_wz(-1, 3)
+    for dx in (0, 3, 1, 2):
+        take_ay(dx, 2)
+    take_bx(1, True)
+    take_bx(2, True)
+    for far in (3, 4):
+        take_bx(far, False)
+        take_bx(far, True)
+    take_wz(1, 4)
     net.wait("mod", mod.at[other], sibling)
     net.wait("size", sizes.at[other], sibling)
-    take_wz(1, 2)
-    take_wz(-1, 2)
-
-    take_ay((3, 4))
+    settle(0)
     settle(1)
     project(pairs[0], True)
-    take_wz(1, 3)
-    take_wz(-1, 3)
     settle(2)
     project(pairs[1], False)
-    take_wz(1, 4)
+    for far in (3, 4):
+        for dx in (0, 3, 1, 2):
+            take_ay(dx, far)
 
     for way, zs in ((1, slice(0, ZN // 2)), (-1, slice(ZN // 2, ZN))):
         net.send("wx", "wx", wt.at[near, zs, core], wt.at[near, zs, core], at_seg(way, 0))

time: 63.9 us -> 61.3 us (0.959)
  Pallas kernels: 61.3 us -> 58.7 us
    pallas_call x1, Pallas kernels: 61.3 us -> 58.7 us  [shards(): pl.pallas_call(kernel, out_shape=jax.ShapeDtypeStruct((ROWS, D), BF16), i...]
where the time goes in v5:
time: 61.3 us; the launch traced here: 61.1 us
  Pallas kernels  58.7 us (96%)
  local copies, waits for them, and re-layouts  1.77 us (3%)
  between operations  0.66 us (1%)
    pallas_call x1, Pallas kernels, shards(): pl.pallas_call(kernel, out_shape=jax.ShapeDtypeStruct((ROWS, D), BF16), i...  58.7 us
    unnamed x1, local copies, waits for them, and re-layouts  1.77 us

profile of v5, /device:TPU:1, one launch (start us, length us, event | category | flops | bytes accessed | tf_op | source)
XLA Modules:
  0.0 61.1 jit_solution(4058823090773434788)
XLA Ops:
  0.7 58.7 %shard_map.91 = bf16[128,1536]{1,0:T(8,128)(2,1)} custom-call(bf16[1,128,1536]{2,1,0:T(8,128)(2,1)} %traj_hbm.1, bf16[128,1536]{1,0:T(8,128)(2,1)} %noise_hbm.1, f32[1,1536]{1,0:T(1,128)} %shift_hbm.1, f32[1,1536]{1,0:T(1,128)} %scale_hbm.1, f32[1]{0:T(128)S(6)} %copy.11.size, f32[8,1536]{1,0:T(8,128)} %table_hbm.1, s32[1,128]{1,0:T(1,128)} %bitcast.5, ...), custom_call_target="tpu_custom_call" | custom-call | tf_op jit(solution)/shard_map/pallas_call | solution.py:395
  59.3 1.8 %copy.12 = bf16[1,128,1536]{2,1,0:T(8,128)(2,1)} copy(bf16[1,128,1536]{2,1,0:T(8,128)(2,1)} %bitcast.3) | data formatting | bytes 786432

commit v6 on v5

--- a/solution.py
+++ b/solution.py
@@ -21,7 +21,7 @@
 SLOT = 32
 WO = D // STEPS
 PAIR = 2 * XN * BLOCK
-SENDS, RECVS = 11, 85
+SENDS, RECVS = 11, 89
 
 
 def dot(a, b, contract=((1,), (0,)), precision=None):
@@ -57,9 +57,9 @@
 
 
 def kernel(
-    traj_hbm, noise_hbm, shift_hbm, scale_hbm, size, table_hbm, pmap_hbm, wq_hbm, wo_hbm, out,
-    traj, noise, shift, scale, table, pmap, wq, stage, shard, slots, perm, w, wt, mod, sizes,
-    sum_q, sum_kv, q, k, v, own_t, parts, sums, before, give, full, extra, start, load, send, recv,
+    traj_hbm, noise_hbm, shift_hbm, scale_hbm, size_hbm, table_hbm, pmap_hbm, wq_hbm, wo_hbm, out,
+    traj, noise, shift, scale, size, table, pmap, wq, stage, shard, slots, perm, w, wt, mod, sizes,
+    sum_q, sum_kv, q, k, v, own_t, parts, sums, before, give, full, extra, start, mask, load, send, recv,
 ):
     seg, step = lax.axis_index("seg"), lax.axis_index("step")
     x, y, core, z = lax.rem(seg, XN), lax.div(seg, XN), lax.rem(step, 2), lax.div(step, 2)
@@ -95,6 +95,7 @@
     sources = [
         (wq_hbm, wq), (traj_hbm, traj), (pmap_hbm, pmap), (table_hbm, table), (shift_hbm, shift), (scale_hbm, scale),
         (wo_hbm.at[:, pl.ds(pl.multiple_of(near * HALF, HALF), HALF)], wt_block(0)), (noise_hbm, noise),
+        (size_hbm, size),
     ]
     loads = [pltpu.make_async_copy(src, dst, load.at[i]) for i, (src, dst) in enumerate(sources)]
     for copy in loads:
@@ -146,7 +147,7 @@
     spread = jnp.mean(jnp.square(inputs), axis=-1, keepdims=True)
     normed = inputs * lax.rsqrt(spread + 1e-06)
     mod[core, mine, :] = (normed * (1.0 + scale[...]) + shift[...]).astype(BF16)
-    sizes[core] = jnp.full((8, 128), size[0], F32)
+    sizes[core] = jnp.broadcast_to(size[...], (8, 128))
     net.send("mod", "up", mod.at[core, high], mod.at[core, first], following)
     net.send("mod", "down", mod.at[core, low], mod.at[core, last], preceding)
     net.send("mod", "mod", mod.at[core, mine], mod.at[core, mine], sibling)
@@ -158,6 +159,11 @@
     j = lax.broadcasted_iota(jnp.int32, shape, 1) - third * SLOT - (i - third * SHARD)
     for c in range(CHUNKS):
         perm[c * BLOCK : (c + 1) * BLOCK, :] = jnp.where(j == c * SHARD, 1.0, 0.0).astype(BF16)
+    at_q = lax.broadcasted_iota(jnp.int32, (ROWS, KEYS), 0)
+    at_k = lax.broadcasted_iota(jnp.int32, (ROWS, KEYS), 1)
+    frame = seg * ROWS - HALO + at_k
+    allowed = (at_k >= at_q) & (at_k <= at_q + 2 * HALO) & (frame >= 0) & (frame < SEGS * ROWS)
+    mask[...] = jnp.where(allowed, 0.0, -1e30).astype(F32)
     net.wait("z", slots.at[0 : STEPS - 1], sibling)
     block = dot(perm[...], slots[...].reshape(STEPS * SLOT, 128)).astype(BF16)
 
@@ -317,12 +323,12 @@
         k[c] = sum_kv[0, :, cols].astype(BF16).reshape(2, KEYS, 128)
         v[c] = sum_kv[1, :, cols].astype(BF16).reshape(2, KEYS, 128)
 
-    at_q = lax.broadcasted_iota(jnp.int32, (ROWS, KEYS), 0)
-    at_k = lax.broadcasted_iota(jnp.int32, (ROWS, KEYS), 1)
-    frame = seg * ROWS - HALO + at_k
-    allowed = (at_k >= at_q) & (at_k <= at_q + 2 * HALO) & (frame >= 0) & (frame < SEGS * ROWS)
-    bias = jnp.where(allowed, 0.0, -1e30).astype(F32)
-    bias = jnp.concatenate([bias, bias], axis=0)
+    share = ROWS // ZN
+
+    def share_rows(i):
+        return pl.ds(pl.multiple_of(i * share, share), share)
+
+    bias = jnp.concatenate([mask[...], mask[...]], axis=0)
     lane = lax.broadcasted_iota(jnp.int32, (ROWS, 128), 1)
     ones = jnp.ones((KEYS, 128), BF16)
     for c in range(3):
@@ -341,36 +347,39 @@
                 total = term
             else:
                 total = total + term
-        give[:, c * 128 : (c + 1) * 128] = total.astype(BF16)
-
-    share = ROWS // ZN
-
-    def share_rows(i):
-        return pl.ds(pl.multiple_of(i * share, share), share)
+        cols = slice(c * 128, (c + 1) * 128)
+        give[:, cols] = total.astype(BF16)
+        for dz in (4, 3, 5, 2, 6, 1, 7):
+            there = share_rows(ring(z + dz, ZN))
+            net.send("there", ("there", c), give.at[there, cols], parts.at[z, :, cols], at_z(dz))
+        parts[z, :, cols] = give[share_rows(z), cols]
 
     net.send("own", "own", own_t, extra.at[core], sibling)
-    for dz in (4, 3, 5, 2, 6, 1, 7):
-        net.send("there", "there", give.at[share_rows(ring(z + dz, ZN))], parts.at[z], at_z(dz))
-    parts[z] = give[share_rows(z), :]
+    for c in range(3):
+        cols = slice(c * 128, (c + 1) * 128)
+        net.wait(("there", c), parts.at[0 : ZN - 1, :, cols], sibling)
+        total = jnp.zeros((share, 128), F32)
+        for i in range(ZN):
+            sums[i, :, cols] = total.astype(BF16)
+            total = total + parts[i, :, cols].astype(F32)
+        for dz in (4, 3, 5, 2, 6, 1, 7):
+            there = ring(z + dz, ZN)
+            net.send("back", ("back", c), sums.at[there, :, cols], before.at[share_rows(z), cols], at_z(dz))
+        before[share_rows(z), cols] = sums[z, :, cols]
+
     net.wait("wx", wt.at[1 - near, :, core], sibling)
     net.send("ws", "ws", wt.at[1 - near, :, core], wt.at[1 - near, :, core], sibling)
-    net.wait("there", parts.at[0 : ZN - 1], sibling)
-    total = jnp.zeros((share, HALF), F32)
-    for i in range(ZN):
-        sums[i] = total.astype(BF16)
-        total = total + parts[i].astype(F32)
-    for dz in (4, 3, 5, 2, 6, 1, 7):
-        net.send("back", "back", sums.at[ring(z + dz, ZN)], before.at[share_rows(z)], at_z(dz))
-    before[share_rows(z), :] = sums[z]
     net.wait("ws", wt.at[:, :, other], sibling)
     net.wait("own", extra.at[other], sibling)
     odd = jnp.where(core == 0, jnp.zeros((ROWS, HALF), BF16), extra[other])
     base = dot(odd, wt[other].reshape(D, HALF), ((1,), (1,)))
     odd = jnp.where(core == 0, jnp.zeros((ROWS, HALF), BF16), own_t[...])
     start[...] = noise[...].astype(F32) + base + dot(odd, wt[core].reshape(D, HALF), ((1,), (1,)))
-    net.wait("back", before.at[0 : ROWS - share], sibling)
-
-    net.send("full", "full", before, full.at[core], sibling)
+
+    for c in range(3):
+        cols = slice(c * 128, (c + 1) * 128)
+        net.wait(("back", c), before.at[0 : ROWS - share, cols], sibling)
+        net.send("full", "full", before.at[:, cols], full.at[core, :, cols], sibling)
     start[...] += dot(before[...], wt[core].reshape(D, HALF), ((1,), (1,)))
     net.wait("full", full.at[other], sibling)
     out[...] = (start[...] + dot(full[other], wt[other].reshape(D, HALF), ((1,), (1,)))).astype(BF16)
@@ -390,18 +399,18 @@
 
 def shards(trajectory, noise, mod_shift, mod_scale, step_size, prompt_table, prompt_map, w_qkv, w_out):
     vmem = pl.BlockSpec(memory_space=pltpu.VMEM)
-    smem = pl.BlockSpec(memory_space=pltpu.SMEM)
     hbm = pl.BlockSpec(memory_space=pl.ANY)
     result = pl.pallas_call(
         kernel,
         out_shape=jax.ShapeDtypeStruct((ROWS, D), BF16),
-        in_specs=[hbm, hbm, hbm, hbm, smem, hbm, hbm, hbm, hbm],
+        in_specs=[hbm] * 9,
         out_specs=vmem,
         scratch_shapes=[
             pltpu.VMEM((1, ROWS, D), BF16),
             pltpu.VMEM((ROWS, D), BF16),
             pltpu.VMEM((1, D), F32),
             pltpu.VMEM((1, D), F32),
+            pltpu.VMEM((1, 1), F32),
             pltpu.VMEM((8, D), F32),
             pltpu.VMEM((1, ROWS), jnp.int32),
             pltpu.VMEM((SHARD, 3 * HQ), BF16),
@@ -426,7 +435,8 @@
             pltpu.VMEM((2, ROWS, HALF), BF16),
             pltpu.VMEM((2, ROWS, HALF), BF16),
             pltpu.VMEM((ROWS, D), F32),
-            pltpu.SemaphoreType.DMA((8,)),
+            pltpu.VMEM((ROWS, KEYS), F32),
+            pltpu.SemaphoreType.DMA((9,)),
             pltpu.SemaphoreType.DMA((SENDS,)),
             pltpu.SemaphoreType.DMA((RECVS,)),
         ],
@@ -434,7 +444,7 @@
             collective_id=0, has_side_effects=True, vmem_limit_bytes=60 * 1024 * 1024
         ),
     )(
-        trajectory, noise, mod_shift, mod_scale, step_size, prompt_table,
+        trajectory, noise, mod_shift, mod_scale, step_size.reshape(1, 1), prompt_table,
         prompt_map.reshape(1, ROWS), w_qkv, w_out.T,
     )
     return result[None]

time: 61.3 us -> 60.7 us (level)
  no operation moved by 1% of the time
where the time goes in v6:
time: 60.7 us; the launch traced here: 60.6 us
  Pallas kernels  58.1 us (96%)
  local copies, waits for them, and re-layouts  1.77 us (3%)
  between operations  0.66 us (1%)
    pallas_call x1, Pallas kernels, shards(): pl.pallas_call(kernel, out_shape=jax.ShapeDtypeStruct((ROWS, D), BF16), i...  58.1 us
    unnamed x1, local copies, waits for them, and re-layouts  1.77 us

profile of v6, /device:TPU:1, one launch (start us, length us, event | category | flops | bytes accessed | tf_op | source)
XLA Modules:
  0.0 60.6 jit_solution(6208198586431750841)
XLA Ops:
  0.7 58.1 %shard_map.91 = bf16[128,1536]{1,0:T(8,128)(2,1)} custom-call(bf16[1,128,1536]{2,1,0:T(8,128)(2,1)} %traj_hbm.1, bf16[128,1536]{1,0:T(8,128)(2,1)} %noise_hbm.1, f32[1,1536]{1,0:T(1,128)} %shift_hbm.1, f32[1,1536]{1,0:T(1,128)} %scale_hbm.1, f32[1,1]{1,0:T(1,128)} %bitcast.4.size_hbm, f32[8,1536]{1,0:T(8,128)} %table_hbm.1, s32[1,128]{1,0:T(1,128)} %bitcast.7, ...), custom_call_target="tpu_custom_call" | custom-call | tf_op jit(solution)/shard_map/pallas_call | solution.py:403
  58.8 1.8 %copy.12 = bf16[1,128,1536]{2,1,0:T(8,128)(2,1)} copy(bf16[1,128,1536]{2,1,0:T(8,128)(2,1)} %bitcast.5) | data formatting | bytes 786432

commit v7 on v6

--- a/solution.py
+++ b/solution.py
@@ -395,6 +395,10 @@
     net.sent("back", parts.at[0 : ZN - 1], sibling)
     net.sent("own", own_t, sibling)
     net.sent("full", before, sibling)
+
+
+def hand_over(result, out):
+    out[0] = result[...]
 
 
 def shards(trajectory, noise, mod_shift, mod_scale, step_size, prompt_table, prompt_map, w_qkv, w_out):
@@ -447,7 +451,15 @@
         trajectory, noise, mod_shift, mod_scale, step_size.reshape(1, 1), prompt_table,
         prompt_map.reshape(1, ROWS), w_qkv, w_out.T,
     )
-    return result[None]
+    rows = ROWS // 4
+    return pl.pallas_call(
+        hand_over,
+        grid=(4,),
+        out_shape=jax.ShapeDtypeStruct((1, ROWS, D), BF16),
+        in_specs=[pl.BlockSpec((rows, D), lambda i: (i, 0))],
+        out_specs=pl.BlockSpec((1, rows, D), lambda i: (0, i, 0)),
+        compiler_params=pltpu.CompilerParams(vmem_limit_bytes=60 * 1024 * 1024),
+    )(result)
 
 
 def solution(mesh):

time: 60.7 us -> 62.1 us (1.023)
  Pallas kernels: 58.1 us -> 61.2 us
  local copies, waits for them, and re-layouts: 1.77 us -> 0 us
    pallas_call x0 -> x1, Pallas kernels: none -> 3.1 us  [shards(): pl.pallas_call(hand_over, grid=(4,), out_shape=jax.ShapeDtypeStruct((1, R...]
    unnamed x1 -> x0, local copies, waits for them, and re-layouts: 1.77 us -> none
where the time goes in v7:
time: 62.1 us; the launch traced here: 61.9 us
  Pallas kernels  61.2 us (99%)
  between operations  0.66 us (1%)
    pallas_call x1, Pallas kernels, shards(): pl.pallas_call(kernel, out_shape=jax.ShapeDtypeStruct((ROWS, D), BF16), i...  58.1 us
    pallas_call x1, Pallas kernels, shards(): pl.pallas_call(hand_over, grid=(4,), out_shape=jax.ShapeDtypeStruct((1, R...  3.1 us

profile of v7, /device:TPU:1, one launch (start us, length us, event | category | flops | bytes accessed | tf_op | source)
XLA Modules:
  0.0 61.9 jit_solution(5834940997912859839)
XLA Ops:
  0.7 58.1 %shard_map.91.result = bf16[128,1536]{1,0:T(8,128)(2,1)} custom-call(bf16[1,128,1536]{2,1,0:T(8,128)(2,1)} %traj_hbm.1, bf16[128,1536]{1,0:T(8,128)(2,1)} %noise_hbm.1, f32[1,1536]{1,0:T(1,128)} %shift_hbm.1, f32[1,1536]{1,0:T(1,128)} %scale_hbm.1, f32[1,1]{1,0:T(1,128)} %bitcast.3.size_hbm, f32[8,1536]{1,0:T(8,128)} %table_hbm.1, s32[1,128]{1,0:T(1,128)} %bitcast.5, ...), custom_call_target="tpu_custom_call" | custom-call | tf_op jit(solution)/shard_map/pallas_call | solution.py:407
  58.8 3.1 %shard_map.92 = bf16[1,128,1536]{2,1,0:T(8,128)(2,1)} custom-call(bf16[128,1536]{1,0:T(8,128)(2,1)} %shard_map.91.result), custom_call_target="tpu_custom_call" | custom-call | tf_op jit(solution)/shard_map/pallas_call | solution.py:455
